TPU v7x, 512 devices: a whole 4x4x16 slice. The times are simulated.
512 devices in a mesh: dp: 4 (over x), row: 32 (over z_lo, y), col: 4 (over z_hi, core).
Axes of the slice: x: 4, y: 4, z: 16 (z_hi: 2, z_lo: 8; z = z_hi * 8 + z_lo), core: 2. Of those that a mesh axis runs over, the one named last changes fastest.
Arguments:
- hidden_in: bfloat16 [4, 256, 128, 256], P('dp', 'row', 'col'), may hold values from -6 to 6
- token_ids: int32 [4, 256, 128], P('dp', 'row', 'col'), may hold values from 0 to 3
- embed: bfloat16 [4, 256], replicated, may hold values from -4 to 4
- norm1_gain: float32 [256], replicated, may hold values from 0.1 to 1.9
- norm2_gain: float32 [256], replicated, may hold values from 0.1 to 1.9
- w_qkv: bfloat16 [256, 768], replicated, may hold values from -0.375 to 0.375
- rel_bias: float32 [8, 225], replicated, may hold values from -3 to 3
- w_proj: bfloat16 [256, 256], replicated, may hold values from -0.375 to 0.375
- w_up: bfloat16 [256, 1024], replicated, may hold values from -0.375 to 0.375
- w_down: bfloat16 [1024, 256], replicated, may hold values from -0.1875 to 0.1875
- out_grad: bfloat16 [4, 256, 128, 256], P('dp', 'row', 'col'), may hold values from -6 to 6
Outputs:
- in_grad: bfloat16 [4, 256, 128, 256], P('dp', 'row', 'col')
- attention_grads: float32 [2048, 128], P(('dp', 'row', 'col'))
- mlp_grads: float32 [4096, 128], P(('dp', 'row', 'col'))
All inputs are finite; a program needn't handle non-finite values.
Results may differ from a plain program's by a relative error of at most 0.0079.
Values may be sent and summed in bfloat16 or wider, within the bound.
A program may use at most 64 MiB of HBM per device.

v0:
```python
import jax
import jax.numpy as jnp
from jax import lax
from jax.sharding import PartitionSpec as P

D = 256
HEADS = 8
VOCAB = 4
WIN = 8
HEAD_DIM = 32
SHIFT = 4
PAIRS = 225


NORM_EPS = 1e-05
GELU_SCALE = 0.7978845608028654
GELU_CUBIC = 0.044715


def passed_along(block, axis, distance):
    devices = range(lax.axis_size(axis))
    route = [((i - distance) % len(devices), i) for i in devices]
    return lax.ppermute(block, axis, route)


def layer_norm(values, gain_vec):
    center = values - jnp.mean(values, axis=-1, keepdims=True)
    inv_std = lax.rsqrt(jnp.mean(center * center, axis=-1, keepdims=True) + NORM_EPS)
    normed = center * inv_std
    return (normed, inv_std, normed * gain_vec)


def norm_back(upstream, normed, inv_std, gain_vec):
    scaled = upstream * gain_vec
    return inv_std * (
        scaled
        - jnp.mean(scaled, axis=-1, keepdims=True)
        - normed * jnp.mean(scaled * normed, axis=-1, keepdims=True)
    )


def gelu_value(pre_act):
    inner_arg = GELU_SCALE * (pre_act + GELU_CUBIC * pre_act * pre_act * pre_act)
    return 0.5 * pre_act * (1.0 + jnp.tanh(inner_arg))


def gelu_slope(pre_act):
    tanh_part = jnp.tanh(GELU_SCALE * (pre_act + GELU_CUBIC * pre_act * pre_act * pre_act))
    return 0.5 * (1.0 + tanh_part) + 0.5 * pre_act * (1.0 - tanh_part * tanh_part) * GELU_SCALE * (
        1.0 + 3.0 * GELU_CUBIC * pre_act * pre_act
    )


def to_windows(grid_map):
    shot_count, height, breadth, channels = grid_map.shape
    blocks = grid_map.reshape(shot_count, height // WIN, WIN, breadth // WIN, WIN, channels)
    return blocks.transpose(0, 1, 3, 2, 4, 5).reshape(-1, WIN * WIN, channels)


def from_windows(window_rows, shot_count, height, breadth):
    channels = window_rows.shape[-1]
    blocks = window_rows.reshape(shot_count, height // WIN, breadth // WIN, WIN, WIN, channels)
    return blocks.transpose(0, 1, 3, 2, 4, 5).reshape(shot_count, height, breadth, channels)


def split_heads(window_rows, first_col):
    window_count = window_rows.shape[0]
    return window_rows[:, :, first_col : first_col + D].reshape(
        window_count, WIN * WIN, HEADS, HEAD_DIM
    )


def position_bias(rel_bias):
    cell_ids = jnp.arange(WIN * WIN)
    cell_row = cell_ids // WIN
    cell_col = cell_ids % WIN
    offset = (cell_row[:, None] - cell_row[None, :] + WIN - 1) * (2 * WIN - 1) + (
        cell_col[:, None] - cell_col[None, :] + WIN - 1
    )
    pair_table = (offset.reshape(1, -1) == jnp.arange(PAIRS)[:, None]).astype(jnp.float32)
    full_bias = jnp.dot(rel_bias, pair_table, precision=lax.Precision.HIGHEST)
    return full_bias.reshape(HEADS, WIN * WIN, WIN * WIN)


def attend(tile_grid, w_qkv, bias_full):
    shot_count, height, breadth, channels = tile_grid.shape
    mixed_rows = jnp.dot(
        tile_grid.reshape(-1, channels), w_qkv, preferred_element_type=jnp.float32
    ).astype(jnp.bfloat16)
    window_rows = to_windows(mixed_rows.reshape(shot_count, height, breadth, 3 * channels))
    queries = split_heads(window_rows, 0)
    key_rows = split_heads(window_rows, D)
    value_rows = split_heads(window_rows, 2 * D)
    scale_factor = HEAD_DIM ** (-0.5)
    scores = (
        jnp.einsum("wihd,wjhd->whij", queries, key_rows, preferred_element_type=jnp.float32)
        * scale_factor
        + bias_full[None]
    )
    raised = jnp.exp(scores)
    soft_probs = raised / jnp.sum(raised, axis=-1, keepdims=True)
    probs_low = soft_probs.astype(jnp.bfloat16)
    context = jnp.einsum(
        "whij,wjhd->wihd", probs_low, value_rows, preferred_element_type=jnp.float32
    )
    context = context.reshape(-1, WIN * WIN, D).astype(jnp.bfloat16)
    return (
        from_windows(context, shot_count, height, breadth),
        (queries, key_rows, value_rows, soft_probs, probs_low),
    )


def attend_back(grad_grid, saved_state):
    shot_count, height, breadth, channels = grad_grid.shape
    queries, key_rows, value_rows, soft_probs, probs_low = saved_state
    grad_heads = to_windows(grad_grid).reshape(-1, WIN * WIN, HEADS, HEAD_DIM)
    grad_dots = jnp.einsum(
        "wihd,wjhd->whij", grad_heads, value_rows, preferred_element_type=jnp.float32
    )
    grad_values = jnp.einsum(
        "whij,wihd->wjhd", probs_low, grad_heads, preferred_element_type=jnp.float32
    )
    grad_scores = soft_probs * (grad_dots - jnp.sum(soft_probs * grad_dots, axis=-1, keepdims=True))
    scores_low = grad_scores.astype(jnp.bfloat16)
    scale_factor = HEAD_DIM ** (-0.5)
    grad_queries = (
        jnp.einsum("whij,wjhd->wihd", scores_low, key_rows, preferred_element_type=jnp.float32)
        * scale_factor
    )
    grad_keys = (
        jnp.einsum("whij,wihd->wjhd", scores_low, queries, preferred_element_type=jnp.float32)
        * scale_factor
    )
    window_count = grad_heads.shape[0]
    joined = jnp.concatenate(
        [
            grad_queries.reshape(window_count, WIN * WIN, D),
            grad_keys.reshape(window_count, WIN * WIN, D),
            grad_values.reshape(window_count, WIN * WIN, D),
        ],
        axis=-1,
    ).astype(jnp.bfloat16)
    return from_windows(joined, shot_count, height, breadth)


def from_ahead(grid_map):
    lower_rows = passed_along(grid_map[:, :SHIFT], "row", -1)
    tall_tile = jnp.concatenate([grid_map[:, SHIFT:], lower_rows], axis=1)
    right_cols = passed_along(tall_tile[:, :, :SHIFT], "col", -1)
    return jnp.concatenate([tall_tile[:, :, SHIFT:], right_cols], axis=2)


def to_behind(tile_grid):
    left_cols = passed_along(tile_grid[:, :, -SHIFT:], "col", 1)
    wide_tile = jnp.concatenate([left_cols, tile_grid[:, :, :-SHIFT]], axis=2)
    upper_rows = passed_along(wide_tile[:, -SHIFT:], "row", 1)
    return jnp.concatenate([upper_rows, wide_tile[:, :-SHIFT]], axis=1)


def on_device(
    hidden_in,
    token_ids,
    embed,
    norm1_gain,
    norm2_gain,
    w_qkv,
    rel_bias,
    w_proj,
    w_up,
    w_down,
    out_grad,
):
    shot_count, height, breadth, channels = hidden_in.shape
    cell_count = shot_count * height * breadth
    token_picks = (token_ids.reshape(-1, 1) == jnp.arange(VOCAB)[None, :]).astype(jnp.bfloat16)
    resid_in = hidden_in.reshape(cell_count, channels).astype(jnp.float32) + jnp.dot(
        token_picks, embed, preferred_element_type=jnp.float32
    )
    normed_one, inv_one, scaled_one = layer_norm(resid_in, norm1_gain)
    normal_low = scaled_one.astype(jnp.bfloat16)
    grid_low = normal_low.reshape(shot_count, height, breadth, channels)
    bias_full = position_bias(rel_bias)
    context_tile, saved_state = attend(from_ahead(grid_low), w_qkv, bias_full)
    context = to_behind(context_tile)
    context_flat = context.reshape(cell_count, channels)
    resid_mid = resid_in + jnp.dot(context_flat, w_proj, preferred_element_type=jnp.float32)
    normed_two, inv_two, scaled_two = layer_norm(resid_mid, norm2_gain)
    mlp_in = scaled_two.astype(jnp.bfloat16)
    pre_act = jnp.dot(mlp_in, w_up, preferred_element_type=jnp.float32)
    activation = gelu_value(pre_act).astype(jnp.bfloat16)
    grad_flat = out_grad.reshape(cell_count, channels)
    grad_act = jnp.einsum("tc,fc->tf", grad_flat, w_down, preferred_element_type=jnp.float32)
    grad_pre = (grad_act * gelu_slope(pre_act)).astype(jnp.bfloat16)
    up_grad = jnp.einsum("tc,tf->cf", mlp_in, grad_pre, preferred_element_type=jnp.float32)
    down_grad = jnp.einsum("tf,tc->fc", activation, grad_flat, preferred_element_type=jnp.float32)
    mlp_local = jnp.concatenate([up_grad.reshape(-1), down_grad.reshape(-1)]).reshape(-1, 128)
    grad_mid = jnp.einsum("tf,cf->tc", grad_pre, w_up, preferred_element_type=jnp.float32)
    grad_res = grad_flat.astype(jnp.float32) + norm_back(grad_mid, normed_two, inv_two, norm2_gain)
    grad_res_low = grad_res.astype(jnp.bfloat16)
    proj_grad = jnp.einsum(
        "tc,te->ce", context_flat, grad_res_low, preferred_element_type=jnp.float32
    )
    grad_context = jnp.einsum(
        "te,ce->tc", grad_res_low, w_proj, preferred_element_type=jnp.float32
    ).astype(jnp.bfloat16)
    grad_grid = grad_context.reshape(shot_count, height, breadth, channels)
    grad_mixed = to_behind(attend_back(from_ahead(grad_grid), saved_state))
    grad_mixed_flat = grad_mixed.reshape(cell_count, 3 * channels)
    qkv_grad = jnp.einsum(
        "tc,tm->cm", normal_low, grad_mixed_flat, preferred_element_type=jnp.float32
    )
    grad_norm_in = jnp.einsum(
        "tm,cm->tc", grad_mixed_flat, w_qkv, preferred_element_type=jnp.float32
    )
    grad_in = grad_res + norm_back(grad_norm_in, normed_one, inv_one, norm1_gain)
    attn_local = jnp.concatenate([qkv_grad.reshape(-1), proj_grad.reshape(-1)]).reshape(-1, 128)
    devices = lax.axis_size(("dp", "row", "col"))
    attn_share = attn_local.shape[0] // devices
    joined = jnp.concatenate(
        [attn_local.reshape(devices, attn_share, 128), mlp_local.reshape(devices, -1, 128)], axis=1
    ).reshape(-1, 128)
    summed = lax.psum_scatter(joined, ("dp", "row", "col"), scatter_dimension=0, tiled=True)
    attention_grads = summed[:attn_share]
    mlp_grads = summed[attn_share:]
    grad_out = grad_in.astype(jnp.bfloat16).reshape(shot_count, height, breadth, channels)
    return (grad_out, attention_grads, mlp_grads)


def solution(mesh):
    placed = (
        P("dp", "row", "col", None),
        P("dp", "row", "col"),
        P(),
        P(),
        P(),
        P(),
        P(),
        P(),
        P(),
        P(),
        P("dp", "row", "col", None),
    )
    return jax.shard_map(
        on_device,
        mesh=mesh,
        in_specs=placed,
        out_specs=(
            P("dp", "row", "col", None),
            P(("dp", "row", "col"), None),
            P(("dp", "row", "col"), None),
        ),
        check_vma=False,
    )
```

profile of v0, /device:TPU:1, one launch (start us, length us, event | category | flops | bytes accessed | tf_op | source)
XLA Modules:
  0.0 627.1 jit_solution(15624194670259918923)
XLA Ops:
  11.0 16.2 %collective-permute-start = (bf16[1,4,32,256]{3,2,1,0:T(8,128)(2,1)S(1)}, bf16[1,4,32,256]{3,2,1,0:T(8,128)(2,1)S(1)}, u32[]{:S(2)}, u32[]{:S(2)}) collective-permute-start(bf16[1,4,32,256]{3,2,1,0:T(8,128)(2,1)S(1)} %get-tuple-element.13), channel_id=1, source_target_pairs={{4,0},{8,4},{12,8},{16,12},{20,16},{24,20},{28,24},{32,28},{36,32}... | collective-permute-start | bytes 196616 | tf_op jit(solution)/shard_map/ppermute | solution.py:23
  27.3 2.0 convolution_bitcast_fusion
  29.6 2.9 collective-permute-start.1
  32.5 10.9 %collective-permute-done.1 = bf16[1,8,4,256]{3,2,1,0:T(4,128)(2,1)S(1)} collective-permute-done((bf16[1,8,4,256]{3,2,1,0:T(4,128)(2,1)S(1)}, bf16[1,8,4,256]{3,2,1,0:T(4,128)(2,1)S(1)}, u32[]{:S(2)}, u32[]{:S(2)}) %collective-permute-start.1) | collective-permute-done | bytes 16416 | tf_op jit(solution)/shard_map/ppermute | solution.py:23
  46.8 1.9 collective-permute-start.2
  49.9 1.9 collective-permute-start.3
  51.8 11.8 %collective-permute-done.3 = bf16[1,4,32,256]{3,2,1,0:T(8,128)(2,1)S(1)} collective-permute-done((bf16[1,4,32,256]{3,2,1,0:T(8,128)(2,1)S(1)}, bf16[1,4,32,256]{3,2,1,0:T(8,128)(2,1)S(1)}, u32[]{:S(2)}, u32[]{:S(2)}) %collective-permute-start.3) | collective-permute-done | bytes 65568 | tf_op jit(solution)/shard_map/ppermute | solution.py:23
  65.3 2.2 fusion.3
  68.4 2.9 collective-permute-start.4
  71.3 2.1 collective-permute-done.4
  73.4 10.9 %collective-permute-start.5 = (bf16[1,8,4,256]{3,2,1,0:T(4,128)(2,1)S(1)}, bf16[1,8,4,256]{3,2,1,0:T(4,128)(2,1)S(1)}, u32[]{:S(2)}, u32[]{:S(2)}) collective-permute-start(bf16[1,8,4,256]{3,2,1,0:T(4,128)(2,1)S(1)} %pad_maximum_fusion.4), channel_id=1, source_target_pairs={{1,0},{2,1},{3,2},{0,3},{5,4},{6,5},{7,6},{4,7},{9,8},{10,9},{11,1... | collective-permute-start | bytes 49160 | tf_op jit(solution)/shard_map/ppermute | solution.py:23
  84.4 5.4 collective-permute-done.5
  90.4 2.8 fusion.7
  94.5 1.6 multiply_reduce_fusion
  100.4 1.9 collective-permute-start.6
  102.4 2.8 fusion.15
  106.0 2.1 collective-permute-start.7
  108.1 2.1 convolution_bitcast_fusion.1
  114.9 6.5 %collective-permute-done.7 = bf16[1,4,32,768]{3,2,1,0:T(8,128)(2,1)} collective-permute-done((bf16[1,4,32,768]{3,2,1,0:T(8,128)(2,1)}, bf16[1,4,32,768]{3,2,1,0:T(8,128)(2,1)}, u32[]{:S(2)}, u32[]{:S(2)}) %collective-permute-start.7) | collective-permute-done | bytes 196640 | tf_op jit(solution)/shard_map/ppermute | solution.py:23
  123.1 2.1 fusion.47
  125.2 2.1 reshape.276
  128.6 2.4 maximum_maximum_fusion
  131.1 4.7 reshape.278
  137.1 480.6 %all-reduce.3.cloned.1.call-done = f32[6144,128]{1,0:T(8,128)} async-done(((f32[6144,128]{1,0:T(8,128)}), f32[6144,128]{1,0:T(8,128)}) %all-reduce.3.cloned.1.call-update) | async-done | bytes 3145744
  (112 shorter events, 29.6 us)
Async XLA Ops:
  7.2 57.0 %copy-start = (bf16[256,1024]{1,0:T(8,128)(2,1)S(1)}, bf16[256,1024]{1,0:T(8,128)(2,1)}, u32[]{:S(2)}) copy-start(bf16[256,1024]{1,0:T(8,128)(2,1)} %param.19) | copy-start | bytes 1572868
  7.2 36.2 %copy-start.5 = (bf16[256,768]{1,0:T(8,128)(2,1)S(1)}, bf16[256,768]{1,0:T(8,128)(2,1)}, u32[]{:S(2)}) copy-start(bf16[256,768]{1,0:T(8,128)(2,1)} %param.16) | copy-start | bytes 1179652
  7.2 610.5 %all-reduce.3.cloned.1.call-start = ((), (), s32[]{:S(2)}) async-start(), calls=%async_computation | async-start | bytes 6291456
  11.0 18.6 %collective-permute-start = (bf16[1,4,32,256]{3,2,1,0:T(8,128)(2,1)S(1)}, bf16[1,4,32,256]{3,2,1,0:T(8,128)(2,1)S(1)}, u32[]{:S(2)}, u32[]{:S(2)}) collective-permute-start(bf16[1,4,32,256]{3,2,1,0:T(8,128)(2,1)S(1)} %get-tuple-element.13), channel_id=1, source_target_pairs={{4,0},{8,4},{12,8},{16,12},{20,16},{24,20},{28,24},{32,28},{36,32}... | collective-permute-start | bytes 196616 | tf_op jit(solution)/shard_map/ppermute | solution.py:23
  29.6 13.8 %collective-permute-start.1 = (bf16[1,8,4,256]{3,2,1,0:T(4,128)(2,1)S(1)}, bf16[1,8,4,256]{3,2,1,0:T(4,128)(2,1)S(1)}, u32[]{:S(2)}, u32[]{:S(2)}) collective-permute-start(bf16[1,8,4,256]{3,2,1,0:T(4,128)(2,1)S(1)} %pad_maximum_fusion.5), channel_id=1, source_target_pairs={{1,0},{2,1},{3,2},{0,3},{5,4},{6,5},{7,6},{4,7},{9,8},{10,9},{11,1... | collective-permute-start | bytes 49160 | tf_op jit(solution)/shard_map/ppermute | solution.py:23
  44.0 2.8 copy-start.11
  44.3 19.3 %copy-start.12 = (bf16[256,256]{1,0:T(8,128)(2,1)S(1)}, bf16[256,256]{1,0:T(8,128)(2,1)}, u32[]{:S(2)}) copy-start(bf16[256,256]{1,0:T(8,128)(2,1)} %param.18) | copy-start | bytes 393220
  45.7 19.5 %copy-start.15 = (bf16[1,8,32,256]{3,2,1,0:T(8,128)(2,1)S(1)}, bf16[1,8,32,256]{3,2,1,0:T(8,128)(2,1)}, u32[]{:S(2)}) copy-start(bf16[1,8,32,256]{3,2,1,0:T(8,128)(2,1)} %param.21) | copy-start | bytes 393220
  46.8 3.1 collective-permute-start.2
  49.9 13.7 %collective-permute-start.3 = (bf16[1,4,32,256]{3,2,1,0:T(8,128)(2,1)S(1)}, bf16[1,4,32,256]{3,2,1,0:T(8,128)(2,1)S(1)}, u32[]{:S(2)}, u32[]{:S(2)}) collective-permute-start(bf16[1,4,32,256]{3,2,1,0:T(8,128)(2,1)S(1)} %fusion.27), channel_id=1, source_target_pairs={{124,0},{0,4},{4,8},{8,12},{12,16},{16,20},{20,24},{24,28},{28,32}... | collective-permute-start | bytes 196616 | tf_op jit(solution)/shard_map/ppermute | solution.py:23
  63.6 1.6 copy-start.8
  64.1 3.3 copy-start.16
  65.2 2.9 copy-start.10
  67.5 22.4 %copy-start.3 = (bf16[256,1024]{1,0:T(8,128)(2,1)}, bf16[256,1024]{1,0:T(8,128)(2,1)S(1)}, u32[]{:S(2)}) copy-start(bf16[256,1024]{1,0:T(8,128)(2,1)S(1)} %fusion.3) | copy-start | bytes 1572868
  68.4 5.0 collective-permute-start.4
  73.4 16.4 %collective-permute-start.5 = (bf16[1,8,4,256]{3,2,1,0:T(4,128)(2,1)S(1)}, bf16[1,8,4,256]{3,2,1,0:T(4,128)(2,1)S(1)}, u32[]{:S(2)}, u32[]{:S(2)}) collective-permute-start(bf16[1,8,4,256]{3,2,1,0:T(4,128)(2,1)S(1)} %pad_maximum_fusion.4), channel_id=1, source_target_pairs={{1,0},{2,1},{3,2},{0,3},{5,4},{6,5},{7,6},{4,7},{9,8},{10,9},{11,1... | collective-permute-start | bytes 49160 | tf_op jit(solution)/shard_map/ppermute | solution.py:23
  94.5 3.8 copy-start.13
  98.6 9.5 %copy-start.4 = (bf16[256,1024]{1,0:T(8,128)(2,1)S(1)}, bf16[256,1024]{1,0:T(8,128)(2,1)}, u32[]{:S(2)}) copy-start(bf16[256,1024]{1,0:T(8,128)(2,1)} %copy-done.3) | copy-start | bytes 1572868
  100.4 4.8 collective-permute-start.6
  105.2 2.8 copy-start.14
  106.0 15.4 %collective-permute-start.7 = (bf16[1,4,32,768]{3,2,1,0:T(8,128)(2,1)}, bf16[1,4,32,768]{3,2,1,0:T(8,128)(2,1)}, u32[]{:S(2)}, u32[]{:S(2)}) collective-permute-start(bf16[1,4,32,768]{3,2,1,0:T(8,128)(2,1)} %fusion.25), channel_id=1, source_target_pairs={{124,0},{0,4},{4,8},{8,12},{12,16},{16,20},{20,24},{24,28},{28,32}... | collective-permute-start | bytes 589832 | tf_op jit(solution)/shard_map/ppermute | solution.py:23
  131.1 4.7 copy-start.2
  131.1 4.7 copy-start.6
  131.1 4.7 copy-start.17
  (3 other events, 2.4 us)
Sparse Core Ops, SparseCore 0:
  135.9 481.8 all-reduce.2
where the time goes:
time: 629 us; the launch traced here: 627 us
  waiting for transfers between devices  518 us (82%)
  starting transfers between devices  40.7 us (6%)
  matrix products  23.3 us (4%)
  local copies, waits for them, and re-layouts  20.4 us (3%)
  between operations  14.7 us (2%)
  other arithmetic  9.51 us (2%)
    unnamed x2, waiting for transfers between devices  481 us
    ppermute x8, starting transfers between devices, passed_along(): return lax.ppermute(block, axis, route)  40.7 us
    ppermute x8, waiting for transfers between devices, passed_along(): return lax.ppermute(block, axis, route)  37.8 us
  transfers between devices with their start and end apart: 9, of which 7 were waited for; matrix products, arithmetic and copies ran while one was open for 2% of the time, Pallas kernels for 0%

commit v1 on v0

v1 whole, which is shorter than its diff:
```python
import jax
import jax.numpy as jnp
from jax import lax
from jax.experimental import pallas as pl
from jax.experimental.pallas import tpu as pltpu
from jax.sharding import PartitionSpec as P

D = 256
FF = 1024
HEADS = 8
HEAD_DIM = 32
WIN = 8
PAIRS = 225
CELLS = 256
NORM_EPS = 1e-05
GELU_SCALE = 0.7978845608028654
GELU_CUBIC = 0.044715
SCALE = HEAD_DIM ** (-0.5)

NX, NY, NZ_LO, NZ_HI = 4, 4, 8, 2
NZ = NZ_LO * NZ_HI
ROW_DEVICES, COL_DEVICES = NZ_LO * NY, NZ_HI * 2
MLP_UNIT, ATT_UNIT = 16, 8

MESH = pl.DeviceIdType.MESH
BF = jnp.bfloat16
F32 = jnp.float32


def iota(shape, dim):
    return lax.broadcasted_iota(jnp.int32, shape, dim)


def one_hot(condition):
    return jnp.where(condition, 1.0, 0.0).astype(BF)


def dot(left, right):
    return jnp.dot(left, right, preferred_element_type=F32)


def dot_nt(left, right):
    return lax.dot_general(left, right, (((1,), (1,)), ((), ())), preferred_element_type=F32)


def dot_tn(left, right):
    return lax.dot_general(left, right, (((0,), (0,)), ((), ())), preferred_element_type=F32)


def mean_of(values):
    return jnp.mean(values, axis=-1, keepdims=True)


def layer_norm(values):
    center = values - mean_of(values)
    inv_std = lax.rsqrt(mean_of(center * center) + NORM_EPS)
    return center * inv_std, inv_std


def norm_back(upstream, normed, inv_std, gain):
    scaled = upstream * gain
    return inv_std * (scaled - mean_of(scaled) - normed * mean_of(scaled * normed))


def window_cell(token):
    return token & 7, ((token >> 6) << 3) + ((token >> 3) & 7)


def block_sum(values, ones_pair):
    high = values.astype(BF)
    low = (values - high.astype(F32)).astype(BF)
    parts = []
    for j in range(4):
        lanes = slice(128 * j, 128 * (j + 1))
        parts.append(dot(jnp.concatenate([high[:, lanes], low[:, lanes]], axis=1), ones_pair))
    return jnp.concatenate(parts, axis=1)


def kernel(
    hid_ref, tok_ref, emb_ref, g1_ref, g2_ref, wqkv_ref, rb_ref, wproj_ref, wup_ref, wdown_ref, og_ref,
    out_ref, att_ref, mlp_ref,
    stage, halo_hid, halo_og, halo_rd, halo_tok,
    bias_s, probs_s, ke_s, ve_s, qkv_s, ctx_s, g_s, df_s, dqkv_s, back_main, back_rd, got_up, got_rd,
    mlp_f32, mlp_send, mlp_recv, mlp_x, mlp_y, mlp_rx, mlp_ry, mlp_x3, mlp_y3, mlp_rx3, mlp_ry3,
    mlp_z, mlp_rz, mlp_c, mlp_rc,
    att_f32, att_send, att_recv, att_x, att_y, att_rx, att_ry, att_x3, att_y3, att_rx3, att_ry3,
    att_z, att_rz, att_c, att_rc,
    halo_ss, halo_rs, back_ss, back_rs, mlp_ss, mlp_rs, att_ss, att_rs, mlp_zs, mlp_zr, att_zs, att_zr,
):
    x_at, row, col = lax.axis_index("dp"), lax.axis_index("row"), lax.axis_index("col")
    z_lo, y_at = row // NY, row % NY
    z_hi, core = col // 2, col % 2
    z_at = z_hi * NZ_LO + z_lo
    mate = 1 - core

    above = (row + ROW_DEVICES - 1) % ROW_DEVICES
    below = (row + 1) % ROW_DEVICES
    left = (col + COL_DEVICES - 1) % COL_DEVICES
    right = (col + 1) % COL_DEVICES

    def at_mate():
        return (x_at, row, z_hi * 2 + mate)

    def at_x(other):
        return (other, row, col)

    def at_y(other):
        return (x_at, z_lo * NY + other, col)

    def at_z(other):
        return (x_at, (other % NZ_LO) * NY + y_at, (other // NZ_LO) * 2 + core)

    partners = [at_mate()]
    partners += [at_x((x_at + d) % NX) for d in range(1, NX)]
    partners += [at_y((y_at + d) % NY) for d in range(1, NY)]
    partners += [at_z((z_at + d) % NZ) for d in range(1, NZ)]
    partners += [(x_at, above, col), (x_at, below, col), (x_at, row, left), (x_at, row, right)]
    partners += [(x_at, above, left), (x_at, below, right)]
    barrier = pltpu.get_barrier_semaphore()
    for partner in partners:
        pl.semaphore_signal(barrier, inc=1, device_id=partner, device_id_type=MESH)

    def send(src, dst, send_sem, recv_sem, device):
        copy = pltpu.make_async_remote_copy(
            src_ref=src, dst_ref=dst, send_sem=send_sem, recv_sem=recv_sem,
            device_id=device, device_id_type=MESH,
        )
        copy.start()
        return copy

    r32, s256 = iota((32, CELLS), 0), iota((32, CELLS), 1)
    stage_row = jnp.where(r32 < 16, 4, 0) + ((r32 & 15) >> 2)
    pick = one_hot(s256 == stage_row * 32 + (r32 & 3))
    stage[:, :D] = dot(pick, hid_ref[...]).astype(BF)
    stage[:, D:] = dot(pick, og_ref[...]).astype(BF)

    pl.semaphore_wait(barrier, len(partners))

    to_above, to_left, to_corner = (x_at, above, col), (x_at, row, left), (x_at, above, left)
    halo = []
    for n, (src, dst, device) in enumerate([
        (tok_ref, halo_tok.at[0], to_above),
        (tok_ref, halo_tok.at[1], to_left),
        (tok_ref, halo_tok.at[2], to_corner),
        (stage.at[pl.ds(0, 16)], halo_rd.at[pl.ds(0, 16)], to_left),
        (stage.at[pl.ds(16, 16)], halo_rd.at[pl.ds(16, 16)], to_corner),
        (hid_ref.at[pl.ds(0, 128)], halo_hid, to_above),
        (og_ref.at[pl.ds(0, 128)], halo_og, to_above),
    ]):
        halo.append(send(src, dst, halo_ss.at[n], halo_rs.at[n], device))

    wide_row, wide_lane = iota((128, 512), 0), iota((128, 512), 1)
    pair_sum = jnp.where(
        (wide_row >> 4) == (wide_lane >> 6), (wide_row & 15) + ((wide_lane >> 3) & 7), -1
    )
    rb = rb_ref[...]
    rb_high = rb.astype(BF)
    rb_rest = rb - rb_high.astype(F32)
    rb_mid = rb_rest.astype(BF)
    rb_low = (rb_rest - rb_mid.astype(F32)).astype(BF)
    rb_parts = jnp.concatenate([rb_high, rb_mid, rb_low], axis=0)
    key_row = iota((8, 512), 1) & 7
    for qj in range(8):
        tall = dot(rb_parts, one_hot(pair_sum == qj + 7))
        tall = tall[0:16] + tall[16:32] + tall[32:48]
        rows = jnp.zeros((8, 512), F32)
        for ki in range(8):
            rows = jnp.where(key_row == ki, tall[7 - ki : 15 - ki], rows)
        bias_s[8 * qj : 8 * qj + 8, :] = rows

    t_row, t_col = window_cell(iota((CELLS, CELLS), 0))
    s_lane = iota((CELLS, CELLS), 1)
    pick_main = one_hot((t_col < 28) & (s_lane == 32 * t_row + t_col + 4))
    e_row, e_col = window_cell(iota((CELLS, 32), 0))
    pick_edge = one_hot((e_col >= 28) & (iota((CELLS, 32), 1) == 4 * e_row + e_col - 28))

    for n in range(6):
        halo[n].wait_recv()
    tok = tok_ref[...]
    tok_below, tok_right, tok_corner = halo_tok[0], halo_tok[1], halo_tok[2]
    tok_main = jnp.concatenate(
        [tok[4 + i : 5 + i, :] for i in range(4)] + [tok_below[i : i + 1, :] for i in range(4)], axis=1
    )
    tok_edge = jnp.concatenate(
        [tok_right[4 + i : 5 + i, 0:4] for i in range(4)] + [tok_corner[i : i + 1, 0:4] for i in range(4)],
        axis=1,
    )
    tok_main = jnp.broadcast_to(tok_main.astype(F32), (128, CELLS)).astype(BF)
    tok_edge = jnp.broadcast_to(tok_edge.astype(F32), (128, 32)).astype(BF)
    ids = dot_nt(pick_main, tok_main) + dot_nt(pick_edge, tok_edge)
    ids = jnp.concatenate([ids, ids], axis=1)
    emb = emb_ref[...].astype(F32)
    token_part = jnp.where(
        ids < 1.5,
        jnp.where(ids < 0.5, emb[0:1], emb[1:2]),
        jnp.where(ids < 2.5, emb[2:3], emb[3:4]),
    )
    main_hid = jnp.concatenate([hid_ref[128:256, :], halo_hid[...]], axis=0)
    resid_in = dot(pick_main, main_hid) + dot(pick_edge, halo_rd[:, :D]) + token_part
    normed_one, inv_one = layer_norm(resid_in)
    gain_one = g1_ref[...]
    normal_low = (normed_one * gain_one).astype(BF)

    qkv_s[...] = dot(normal_low, wqkv_ref[...]).astype(BF)

    head_mask = one_hot((iota((512, D), 0) >> 6) == (iota((512, D), 1) >> 5))
    ones_pair = one_hot(((iota((256, 128), 0) & 127) >> 6) == (iota((256, 128), 1) >> 6))
    for w in range(4):
        cells = slice(64 * w, 64 * w + 64)
        keys = jnp.concatenate([qkv_s[cells, D : 2 * D]] * HEADS, axis=0) * head_mask
        ke_s[w] = keys
        ve_s[w] = jnp.concatenate([qkv_s[cells, 2 * D :]] * HEADS, axis=0) * head_mask
        probs_s[cells, :] = jnp.exp(dot_nt(qkv_s[cells, :D], keys) * SCALE + bias_s[...])
    raised = probs_s[...]
    probs = raised / block_sum(raised, ones_pair)
    probs_s[...] = probs
    probs_low = probs.astype(BF)
    for w in range(4):
        cells = slice(64 * w, 64 * w + 64)
        ctx_s[cells, :] = dot(probs_low[cells], ve_s[w]).astype(BF)

    context = ctx_s[...]
    resid_mid = resid_in + dot(context, wproj_ref[...])
    normed_two, inv_two = layer_norm(resid_mid)
    gain_two = g2_ref[...]
    mlp_in = (normed_two * gain_two).astype(BF)

    halo[6].wait_recv()
    main_og = jnp.concatenate([og_ref[128:256, :], halo_og[...]], axis=0)
    grad_f32 = dot(pick_main, main_og) + dot(pick_edge, halo_rd[:, D:])
    grad = grad_f32.astype(BF)

    grad_mid = jnp.zeros((CELLS, D), F32)
    for n in range(4):
        units = slice(256 * n, 256 * n + 256)
        pre = dot(mlp_in, wup_ref[:, units])
        grad_act = dot_nt(grad, wdown_ref[units, :])
        square = pre * pre
        tanh_part = jnp.tanh(GELU_SCALE * pre * (1.0 + GELU_CUBIC * square))
        half_plus = 0.5 * (1.0 + tanh_part)
        slope = half_plus + 0.5 * pre * (1.0 - tanh_part * tanh_part) * (
            GELU_SCALE * (1.0 + 3.0 * GELU_CUBIC * square)
        )
        act = (pre * half_plus).astype(BF)
        grad_pre = (grad_act * slope).astype(BF)
        grad_mid = grad_mid + dot_nt(grad_pre, wup_ref[:, units])
        up_grad = dot_tn(mlp_in, grad_pre)
        half, lane_tile = n // 2, 2 * (n % 2)
        mlp_f32[half, pl.ds(lane_tile, 256, stride=4), :] = up_grad[:, :128]
        mlp_f32[half, pl.ds(lane_tile + 1, 256, stride=4), :] = up_grad[:, 128:]
        down_grad = dot_tn(act, grad)
        mlp_f32[0, 1024 + 256 * n : 1280 + 256 * n, :] = down_grad[:, :128]
        mlp_f32[1, 1024 + 256 * n : 1280 + 256 * n, :] = down_grad[:, 128:]

    mlp = dict(
        unit=MLP_UNIT, f32=mlp_f32, send=mlp_send, recv=mlp_recv, x=mlp_x, y=mlp_y, rx=mlp_rx, ry=mlp_ry,
        x3=mlp_x3, y3=mlp_y3, rx3=mlp_rx3, ry3=mlp_ry3, z=mlp_z, rz=mlp_rz, c=mlp_c, rc=mlp_rc,
        ss=mlp_ss, rs=mlp_rs, zs=mlp_zs, zr=mlp_zr,
    )
    att = dict(
        unit=ATT_UNIT, f32=att_f32, send=att_send, recv=att_recv, x=att_x, y=att_y, rx=att_rx, ry=att_ry,
        x3=att_x3, y3=att_y3, rx3=att_rx3, ry3=att_ry3, z=att_z, rz=att_rz, c=att_c, rc=att_rc,
        ss=att_ss, rs=att_rs, zs=att_zs, zr=att_zr,
    )
    sends = []

    def start_mate(b):
        b["send"][...] = b["f32"][mate].astype(BF)
        b["p1"] = [send(b["send"], b["recv"], b["ss"].at[0], b["rs"].at[0], at_mate())]
        sends.extend(b["p1"])

    def start_xy(b):
        b["p1"][0].wait_recv()
        unit = b["unit"]
        part = NZ_LO // 2 * NY * unit
        for x in range(NX):
            first, second = slice(2 * part * x, 2 * part * x + part), slice(2 * part * x + part, 2 * part * (x + 1))
            total = b["f32"][core, first, :] + b["recv"][first, :].astype(F32)
            b["x"][x] = total.astype(BF)
            total = b["f32"][core, second, :] + b["recv"][second, :].astype(F32)
            total = total.reshape(NZ_LO // 2, NY, unit, 128)
            quarter = part // NY
            for y in range(NY):
                b["y"][y, quarter * x : quarter * (x + 1), :] = total[:, y].reshape(quarter, 128).astype(BF)
        b["p2"] = []
        for d in range(1, NX):
            other = (x_at + d) % NX
            b["p2"].append(
                send(b["x"].at[other], b["rx"].at[d - 1], b["ss"].at[d], b["rs"].at[d], at_x(other))
            )
            other = (y_at + d) % NY
            b["p2"].append(
                send(b["y"].at[other], b["ry"].at[d - 1], b["ss"].at[3 + d], b["rs"].at[3 + d], at_y(other))
            )
        sends.extend(b["p2"])

    def start_yx(b):
        for copy in b["p2"]:
            copy.wait_recv()
        unit = b["unit"]
        quarter = NZ_LO // 2 * unit
        total = b["x"][x_at].astype(F32)
        for d in range(NX - 1):
            total = total + b["rx"][d].astype(F32)
        total = total.reshape(NZ_LO // 2, NY, unit, 128)
        for y in range(NY):
            b["x3"][y] = total[:, y].reshape(quarter, 128).astype(BF)
        total = b["y"][y_at].astype(F32)
        for d in range(NY - 1):
            total = total + b["ry"][d].astype(F32)
        for x in range(NX):
            b["y3"][x] = total[quarter * x : quarter * (x + 1)].astype(BF)
        b["p3"] = []
        for d in range(1, NX):
            other = (y_at + d) % NY
            b["p3"].append(
                send(b["x3"].at[other], b["rx3"].at[d - 1], b["ss"].at[6 + d], b["rs"].at[6 + d], at_y(other))
            )
            other = (x_at + d) % NX
            b["p3"].append(
                send(b["y3"].at[other], b["ry3"].at[d - 1], b["ss"].at[9 + d], b["rs"].at[9 + d], at_x(other))
            )
        sends.extend(b["p3"])

    def start_z(b):
        for copy in b["p3"]:
            copy.wait_recv()
        unit = b["unit"]
        for part, own, own_at, got in ((0, b["x3"], y_at, b["rx3"]), (1, b["y3"], x_at, b["ry3"])):
            total = own[own_at].astype(F32)
            for d in range(NX - 1):
                total = total + got[d].astype(F32)
            piece = unit // 2
            for lo in range(NZ_LO // 2):
                for hi in range(NZ_HI):
                    start = lo * unit + hi * piece
                    b["z"][part * (NZ_LO // 2) + lo, hi] = total[start : start + piece]
        b["p4"] = []
        for d in range(1, NZ):
            other = (z_at + d) % NZ
            b["p4"].append(
                send(
                    b["z"].at[other % NZ_LO, other // NZ_LO], b["rz"].at[d - 1],
                    b["zs"].at[d - 1], b["zr"].at[d - 1], at_z(other),
                )
            )
        sends.extend(b["p4"])

    def start_last(b):
        for copy in b["p4"]:
            copy.wait_recv()
        total = b["z"][z_lo, z_hi]
        for d in range(NZ - 1):
            total = total + b["rz"][d]
        rows = b["unit"] // 4
        b["c"][0] = total[:rows]
        b["c"][1] = total[rows:]
        b["p5"] = [send(b["c"].at[mate], b["rc"], b["ss"].at[13], b["rs"].at[13], at_mate())]
        sends.extend(b["p5"])

    def finish(b):
        b["p5"][0].wait_recv()
        own, got = b["c"][core], b["rc"][...]
        return jnp.where(core == 0, own, got), jnp.where(core == 0, got, own)

    start_mate(mlp)

    grad_res = grad_f32 + norm_back(grad_mid, normed_two, inv_two, gain_two)
    grad_res_low = grad_res.astype(BF)
    proj_grad = dot_tn(context, grad_res_low)
    att_f32[0, 768:, :] = proj_grad[:, :128]
    att_f32[1, 768:, :] = proj_grad[:, 128:]
    grad_context = dot_nt(grad_res_low, wproj_ref[...]).astype(BF)

    start_xy(mlp)

    grad_probs = jnp.concatenate(
        [dot_nt(grad_context[64 * w : 64 * w + 64], ve_s[w]) for w in range(4)], axis=0
    )
    probs = probs_s[...]
    grad_scores = probs * (grad_probs - block_sum(probs * grad_probs, ones_pair))
    scores_low = grad_scores.astype(BF)
    probs_low = probs.astype(BF)

    start_yx(mlp)

    head_of_lane = iota((64, D), 1) >> 5

    def own_heads(stacked):
        result = jnp.zeros((64, D), F32)
        for h in range(HEADS):
            result = jnp.where(head_of_lane == h, stacked[64 * h : 64 * h + 64], result)
        return result

    for w in range(4):
        cells = slice(64 * w, 64 * w + 64)
        dqkv_s[cells, :D] = (dot(scores_low[cells], ke_s[w]) * SCALE).astype(BF)
        dqkv_s[cells, D : 2 * D] = (own_heads(dot_tn(scores_low[cells], qkv_s[cells, :D])) * SCALE).astype(BF)
        dqkv_s[cells, 2 * D :] = own_heads(dot_tn(probs_low[cells], grad_context[cells])).astype(BF)

    start_z(mlp)

    for m in range(3):
        part_grad = dot_tn(normal_low, dqkv_s[:, D * m : D * (m + 1)])
        att_f32[0, pl.ds(m, 256, stride=3), :] = part_grad[:, :128]
        att_f32[1, pl.ds(m, 256, stride=3), :] = part_grad[:, 128:]
    start_mate(att)

    grad_norm_in = dot_nt(dqkv_s[...], wqkv_ref[...])
    grad_in = (grad_res + norm_back(grad_norm_in, normed_one, inv_one, gain_one)).astype(BF)
    u_row, u_col = window_cell(iota((CELLS, CELLS), 1))
    place_main = one_hot((u_col < 28) & (iota((CELLS, CELLS), 0) == 32 * u_row + u_col + 4))
    v_row, v_col = window_cell(iota((32, CELLS), 1))
    place_edge = one_hot((v_col >= 28) & (iota((32, CELLS), 0) == 4 * v_row + v_col - 28))
    back_main[...] = dot(place_main, grad_in).astype(BF)
    back_rd[...] = dot(place_edge, grad_in).astype(BF)
    to_below, to_right, to_last = (x_at, below, col), (x_at, row, right), (x_at, below, right)
    back = []
    for n, (src, dst, device) in enumerate([
        (back_rd.at[pl.ds(0, 16)], got_rd.at[pl.ds(0, 16)], to_right),
        (back_rd.at[pl.ds(16, 16)], got_rd.at[pl.ds(16, 16)], to_last),
        (back_main.at[pl.ds(128, 128)], got_up, to_below),
    ]):
        back.append(send(src, dst, back_ss.at[n], back_rs.at[n], device))

    start_xy(att)
    start_last(mlp)

    for copy in back:
        copy.wait_recv()
    spread = one_hot(iota((128, 16), 0) == 32 * (iota((128, 16), 1) >> 2) + (iota((128, 16), 1) & 3))
    out_ref[0:128, :] = (got_up[...].astype(F32) + dot(spread, got_rd[16:32, :])).astype(BF)
    out_ref[128:256, :] = (back_main[0:128, :].astype(F32) + dot(spread, got_rd[0:16, :])).astype(BF)

    start_yx(att)
    start_z(att)
    first, second = finish(mlp)
    apart = jnp.concatenate([first, second], axis=0)
    mixed = jnp.concatenate([part[i : i + 1] for i in range(4) for part in (first, second)], axis=0)
    mlp_ref[...] = jnp.where(x_at < 2, apart, mixed)

    start_last(att)
    first, second = finish(att)
    att_ref[...] = jnp.concatenate([first[0:1], second[0:1], first[1:2], second[1:2]], axis=0)

    for copy in halo + back + sends:
        copy.wait_send()


def reduce_scratch(unit):
    chip_rows = NZ_LO * NY * unit
    half, quarter = chip_rows // 2, chip_rows // 8
    return [
        pltpu.VMEM((2, NX * chip_rows, 128), F32),
        pltpu.VMEM((NX * chip_rows, 128), BF),
        pltpu.VMEM((NX * chip_rows, 128), BF),
        pltpu.VMEM((NX, half, 128), BF),
        pltpu.VMEM((NY, half, 128), BF),
        pltpu.VMEM((NX - 1, half, 128), BF),
        pltpu.VMEM((NY - 1, half, 128), BF),
        pltpu.VMEM((NY, quarter, 128), BF),
        pltpu.VMEM((NX, quarter, 128), BF),
        pltpu.VMEM((NY - 1, quarter, 128), BF),
        pltpu.VMEM((NX - 1, quarter, 128), BF),
        pltpu.VMEM((NZ_LO, NZ_HI, unit // 2, 128), F32),
        pltpu.VMEM((NZ - 1, unit // 2, 128), F32),
        pltpu.VMEM((2, unit // 4, 128), F32),
        pltpu.VMEM((unit // 4, 128), F32),
    ]


def on_device(
    hidden_in, token_ids, embed, norm1_gain, norm2_gain, w_qkv, rel_bias, w_proj, w_up, w_down, out_grad
):
    table = rel_bias.reshape(HEADS, 15, 15).transpose(1, 0, 2)
    table = jnp.pad(table, ((0, 1), (0, 0), (0, 1))).reshape(16, 128)
    dma = pltpu.SemaphoreType.DMA
    grad_out, attention_grads, mlp_grads = pl.pallas_call(
        kernel,
        out_shape=(
            jax.ShapeDtypeStruct((CELLS, D), BF),
            jax.ShapeDtypeStruct((4, 128), F32),
            jax.ShapeDtypeStruct((8, 128), F32),
        ),
        in_specs=[pl.BlockSpec(memory_space=pltpu.VMEM)] * 11,
        out_specs=[pl.BlockSpec(memory_space=pltpu.VMEM)] * 3,
        scratch_shapes=[
            pltpu.VMEM((32, 2 * D), BF),
            pltpu.VMEM((128, D), BF),
            pltpu.VMEM((128, D), BF),
            pltpu.VMEM((32, 2 * D), BF),
            pltpu.VMEM((3, 8, 32), jnp.int32),
            pltpu.VMEM((64, 512), F32),
            pltpu.VMEM((CELLS, 512), F32),
            pltpu.VMEM((4, 512, D), BF),
            pltpu.VMEM((4, 512, D), BF),
            pltpu.VMEM((CELLS, 3 * D), BF),
            pltpu.VMEM((CELLS, D), BF),
            pltpu.VMEM((CELLS, FF), BF),
            pltpu.VMEM((CELLS, FF), BF),
            pltpu.VMEM((CELLS, 3 * D), BF),
            pltpu.VMEM((CELLS, D), BF),
            pltpu.VMEM((32, D), BF),
            pltpu.VMEM((128, D), BF),
            pltpu.VMEM((32, D), BF),
        ]
        + reduce_scratch(MLP_UNIT)
        + reduce_scratch(ATT_UNIT)
        + [dma((7,)), dma((7,)), dma((3,)), dma((3,)), dma((14,)), dma((14,)), dma((14,)), dma((14,))]
        + [dma((NZ - 1,))] * 4,
        compiler_params=pltpu.CompilerParams(
            collective_id=0, has_side_effects=True, vmem_limit_bytes=48 * 1024 * 1024
        ),
        name="decoder_block_backward",
    )(
        hidden_in.reshape(CELLS, D),
        token_ids.reshape(8, 32),
        embed,
        norm1_gain.reshape(1, D),
        norm2_gain.reshape(1, D),
        w_qkv,
        table,
        w_proj,
        w_up,
        w_down,
        out_grad.reshape(CELLS, D),
    )
    return grad_out.reshape(1, 8, 32, D), attention_grads, mlp_grads


def solution(mesh):
    placed = (
        P("dp", "row", "col", None),
        P("dp", "row", "col"),
        P(),
        P(),
        P(),
        P(),
        P(),
        P(),
        P(),
        P(),
        P("dp", "row", "col", None),
    )
    return jax.shard_map(
        on_device,
        mesh=mesh,
        in_specs=placed,
        out_specs=(
            P("dp", "row", "col", None),
            P(("dp", "row", "col"), None),
            P(("dp", "row", "col"), None),
        ),
        check_vma=False,
    )
```

time: 629 us -> 75.6 us (0.12)
  waiting for transfers between devices: 518 us -> 0 us
  Pallas kernels: 0 us -> 66.4 us
  starting transfers between devices: 40.7 us -> 0 us
  matrix products: 23.3 us -> 0 us
  between operations: 14.7 us -> 0.72 us
  local copies, waits for them, and re-layouts: 20.4 us -> 8.14 us
  other arithmetic: 9.51 us -> 0 us
    unnamed x2 -> x0, waiting for transfers between devices: 481 us -> none
    pallas_call x0 -> x1, Pallas kernels: none -> 66.4 us  [on_device(): pl.pallas_call(kernel, out_shape=(jax.ShapeDtypeStruct((CELLS, D), BF), j...]
    ppermute x8 -> x0, starting transfers between devices: 40.7 us -> none  [passed_along(): return lax.ppermute(block, axis, route)]
    ppermute x8 -> x0, waiting for transfers between devices: 37.8 us -> none  [passed_along(): return lax.ppermute(block, axis, route)]
    dot_general x19 -> x0, matrix products: 21.7 us -> none  [the longest x1 2.84 us: on_device(): jnp.einsum('tf,tc->fc', activation, grad_flat, preferred_element_type=jnp...]
    reshape x3 -> x2, local copies, waits for them, and re-layouts: 6.77 us -> 0.16 us  [the longest x1 0.08 us: on_device(): table = jnp.pad(table, ((0, 1), (0, 0), (0, 1))).reshape(16, 128)]
  transfers between devices with their start and end apart: 9 -> 0, of which waited for: 7 -> 0; matrix products, arithmetic and copies ran while one was open for 2% -> 0% of each run, Pallas kernels for 0% -> 0%
where the time goes in v1:
time: 75.6 us; the launch traced here: 75.3 us
  Pallas kernels  66.4 us (88%)
  local copies, waits for them, and re-layouts  8.14 us (11%)
    pallas_call x1, Pallas kernels, on_device(): pl.pallas_call(kernel, out_shape=(jax.ShapeDtypeStruct((CELLS, D), BF), j...  66.4 us
    unnamed x26, local copies, waits for them, and re-layouts  7.97 us

profile of v1, /device:TPU:1, one launch (start us, length us, event | category | flops | bytes accessed | tf_op | source)
XLA Modules:
  0.0 75.3 jit_solution(4158261283988239870)
XLA Ops:
  0.6 0.0 copy-start.10
  0.6 0.0 copy-start.2
  0.7 0.7 copy-done.10
  1.3 0.1 reshape.34
  1.5 0.0 copy-start.6
  1.5 0.0 copy-start.7
  1.5 0.0 copy-start.8
  1.5 0.0 copy-start.9
  1.5 0.1 reshape.35.rb_ref
  1.6 0.1 copy-done.2
  1.6 0.5 copy-done.6
  2.2 0.0 copy-done.7
  2.2 0.0 copy-done.8
  2.2 0.0 copy-done.9
  2.2 0.0 copy-start
  2.2 1.0 %copy-done = bf16[256,1024]{1,0:T(8,128)(2,1)S(1)} copy-done((bf16[256,1024]{1,0:T(8,128)(2,1)S(1)}, bf16[256,1024]{1,0:T(8,128)(2,1)}, u32[]{:S(2)}) %copy-start) | copy-done | bytes 524312
  3.3 1.0 %copy-done.1 = bf16[1024,256]{1,0:T(8,128)(2,1)S(1)} copy-done((bf16[1024,256]{1,0:T(8,128)(2,1)S(1)}, bf16[1024,256]{1,0:T(8,128)(2,1)}, u32[]{:S(2)}) %copy-start.1) | copy-done | bytes 524312
  4.3 0.9 %copy-done.3 = bf16[1,8,32,256]{3,2,1,0:T(8,128)(2,1)S(1)} copy-done((bf16[1,8,32,256]{3,2,1,0:T(8,128)(2,1)S(1)}, bf16[1,8,32,256]{3,2,1,0:T(8,128)(2,1)}, u32[]{:S(2)}) %copy-start.3) | copy-done | bytes 131096
  5.2 0.9 %copy-done.4 = bf16[256,256]{1,0:T(8,128)(2,1)S(1)} copy-done((bf16[256,256]{1,0:T(8,128)(2,1)S(1)}, bf16[256,256]{1,0:T(8,128)(2,1)}, u32[]{:S(2)}) %copy-start.4) | copy-done | bytes 131096
  6.1 0.9 %copy-done.5 = bf16[1,8,32,256]{3,2,1,0:T(8,128)(2,1)S(1)} copy-done((bf16[1,8,32,256]{3,2,1,0:T(8,128)(2,1)S(1)}, bf16[1,8,32,256]{3,2,1,0:T(8,128)(2,1)}, u32[]{:S(2)}) %copy-start.5) | copy-done | bytes 131096
  7.0 66.4 %decoder_block_backward.1 = (bf16[256,256]{1,0:T(8,128)(2,1)S(1)}, f32[4,128]{1,0:T(4,128)S(1)}, f32[8,128]{1,0:T(8,128)S(1)}) custom-call(bf16[256,256]{1,0:T(8,128)(2,1)S(1)} %bitcast.7, s32[8,32]{1,0:T(8,128)S(1)} %bitcast.10, bf16[4,256]{1,0:T(4,128)(2,1)S(1)} %copy-done.7, f32[1,256]{1,0:T(1,128)S(1)} %bitcast.11, f32[1,256]{1,0:T(1,128)S(1)} %bitcast.12, ...), custom_call_target="tpu_custom_call" | custom-call | tf_op jit(solution)/shard_map/decoder_block_backward/pallas_call | solution.py:478
  73.5 0.7 copy.20
  74.1 0.6 copy.21
  74.7 0.6 copy.22
  (6 shorter events, 0.0 us)
Async XLA Ops:
  0.6 0.7 copy-start.10
  0.6 1.0 %copy-start.2 = (bf16[256,768]{1,0:T(8,128)(2,1)S(1)}, bf16[256,768]{1,0:T(8,128)(2,1)}, u32[]{:S(2)}) copy-start(bf16[256,768]{1,0:T(8,128)(2,1)} %wqkv_ref.1) | copy-start | bytes 1179652
  1.5 0.7 copy-start.6
  1.5 0.7 copy-start.7
  1.5 0.7 copy-start.8
  1.5 0.7 copy-start.9
  2.2 1.0 %copy-start = (bf16[256,1024]{1,0:T(8,128)(2,1)S(1)}, bf16[256,1024]{1,0:T(8,128)(2,1)}, u32[]{:S(2)}) copy-start(bf16[256,1024]{1,0:T(8,128)(2,1)} %wup_ref.1) | copy-start | bytes 1572868
  3.3 1.0 %copy-start.1 = (bf16[1024,256]{1,0:T(8,128)(2,1)S(1)}, bf16[1024,256]{1,0:T(8,128)(2,1)}, u32[]{:S(2)}) copy-start(bf16[1024,256]{1,0:T(8,128)(2,1)} %wdown_ref.1) | copy-start | bytes 1572868
  4.3 0.9 %copy-start.3 = (bf16[1,8,32,256]{3,2,1,0:T(8,128)(2,1)S(1)}, bf16[1,8,32,256]{3,2,1,0:T(8,128)(2,1)}, u32[]{:S(2)}) copy-start(bf16[1,8,32,256]{3,2,1,0:T(8,128)(2,1)} %param.11) | copy-start | bytes 393220
  5.2 0.9 %copy-start.4 = (bf16[256,256]{1,0:T(8,128)(2,1)S(1)}, bf16[256,256]{1,0:T(8,128)(2,1)}, u32[]{:S(2)}) copy-start(bf16[256,256]{1,0:T(8,128)(2,1)} %wproj_ref.1) | copy-start | bytes 393220
  6.1 0.9 %copy-start.5 = (bf16[1,8,32,256]{3,2,1,0:T(8,128)(2,1)S(1)}, bf16[1,8,32,256]{3,2,1,0:T(8,128)(2,1)}, u32[]{:S(2)}) copy-start(bf16[1,8,32,256]{3,2,1,0:T(8,128)(2,1)} %param.21) | copy-start | bytes 393220

commit v2 on v1

--- a/solution.py
+++ b/solution.py
@@ -76,17 +76,43 @@
     return jnp.concatenate(parts, axis=1)
 
 
+def load_rel_bias(rb):
+    rb_high = rb.astype(BF)
+    rb_rest = rb - rb_high.astype(F32)
+    rb_mid = rb_rest.astype(BF)
+    rb_low = (rb_rest - rb_mid.astype(F32)).astype(BF)
+    parts = jnp.concatenate([rb_high, rb_mid, rb_low], axis=0)
+    pair, lane = iota((PAIRS, 2048), 0), iota((PAIRS, 2048), 1)
+    offset = lane & 15
+    spread = dot(parts, one_hot((offset < 15) & (pair == 15 * (lane >> 7) + offset)))
+    spread = spread[0:8] + spread[8:16] + spread[16:24]
+    own = iota((8, 2048), 0) == ((iota((8, 2048), 1) >> 4) & 7)
+    line = jnp.sum(jnp.where(own, spread, 0.0), axis=0, keepdims=True)
+    return jnp.concatenate([line[:, 128 * u : 128 * u + 128] for u in range(16)], axis=0)
+
+
 def kernel(
+    hid_in, tok_in, emb_in, g1_in, g2_in, wqkv_in, rb_in, wproj_in, wup_in, wdown_in, og_in,
+    out_ref, att_ref, mlp_ref,
     hid_ref, tok_ref, emb_ref, g1_ref, g2_ref, wqkv_ref, rb_ref, wproj_ref, wup_ref, wdown_ref, og_ref,
-    out_ref, att_ref, mlp_ref,
-    stage, halo_hid, halo_og, halo_rd, halo_tok,
-    bias_s, probs_s, ke_s, ve_s, qkv_s, ctx_s, g_s, df_s, dqkv_s, back_main, back_rd, got_up, got_rd,
-    mlp_f32, mlp_send, mlp_recv, mlp_x, mlp_y, mlp_rx, mlp_ry, mlp_x3, mlp_y3, mlp_rx3, mlp_ry3,
-    mlp_z, mlp_rz, mlp_c, mlp_rc,
-    att_f32, att_send, att_recv, att_x, att_y, att_rx, att_ry, att_x3, att_y3, att_rx3, att_ry3,
-    att_z, att_rz, att_c, att_rc,
-    halo_ss, halo_rs, back_ss, back_rs, mlp_ss, mlp_rs, att_ss, att_rs, mlp_zs, mlp_zr, att_zs, att_zr,
+    stage_hid, stage_og, halo_hid, halo_og, edge_hid, edge_og, halo_tok,
+    bias_s, probs_s, ke_s, ve_s, qkv_s, ctx_s, dqkv_s, back_main, back_rd, got_up, got_rd,
+    mlp_f32, mlp_send, mlp_recv, mlp_x, mlp_y, mlp_rx, mlp_ry,
+    att_f32, att_send, att_recv, att_x, att_y, att_rx, att_ry,
+    x3, y3, rx3, ry3, z_send, z_recv, c_send, c_recv,
+    in_sem, halo_ss, halo_rs, back_ss, back_rs, mlp_ss, mlp_rs, att_ss, att_rs, late_ss, late_rs, z_ss, z_rs,
 ):
+    loads = [
+        pltpu.make_async_copy(src, dst, in_sem.at[n])
+        for n, (src, dst) in enumerate([
+            (hid_in, hid_ref), (og_in, og_ref), (tok_in, tok_ref), (rb_in, rb_ref), (emb_in, emb_ref),
+            (g1_in, g1_ref), (g2_in, g2_ref), (wqkv_in, wqkv_ref), (wproj_in, wproj_ref),
+            (wup_in, wup_ref), (wdown_in, wdown_ref),
+        ])
+    ]
+    for load in loads:
+        load.start()
+
     x_at, row, col = lax.axis_index("dp"), lax.axis_index("row"), lax.axis_index("col")
     z_lo, y_at = row // NY, row % NY
     z_hi, core = col // 2, col % 2
@@ -110,12 +136,11 @@
     def at_z(other):
         return (x_at, (other % NZ_LO) * NY + y_at, (other // NZ_LO) * 2 + core)
 
-    partners = [at_mate()]
+    partners = [(x_at, above, left), (x_at, below, right), (x_at, above, col), (x_at, below, col)]
+    partners += [(x_at, row, left), (x_at, row, right), at_mate()]
     partners += [at_x((x_at + d) % NX) for d in range(1, NX)]
     partners += [at_y((y_at + d) % NY) for d in range(1, NY)]
     partners += [at_z((z_at + d) % NZ) for d in range(1, NZ)]
-    partners += [(x_at, above, col), (x_at, below, col), (x_at, row, left), (x_at, row, right)]
-    partners += [(x_at, above, left), (x_at, below, right)]
     barrier = pltpu.get_barrier_semaphore()
     for partner in partners:
         pl.semaphore_signal(barrier, inc=1, device_id=partner, device_id_type=MESH)
@@ -131,29 +156,34 @@
     r32, s256 = iota((32, CELLS), 0), iota((32, CELLS), 1)
     stage_row = jnp.where(r32 < 16, 4, 0) + ((r32 & 15) >> 2)
     pick = one_hot(s256 == stage_row * 32 + (r32 & 3))
-    stage[:, :D] = dot(pick, hid_ref[...]).astype(BF)
-    stage[:, D:] = dot(pick, og_ref[...]).astype(BF)
+    for n in range(3):
+        loads[n].wait()
+    stage_hid[...] = dot(pick, hid_ref[...]).astype(BF)
+    stage_og[...] = dot(pick, og_ref[...]).astype(BF)
 
     pl.semaphore_wait(barrier, len(partners))
 
     to_above, to_left, to_corner = (x_at, above, col), (x_at, row, left), (x_at, above, left)
     halo = []
     for n, (src, dst, device) in enumerate([
+        (stage_hid.at[pl.ds(16, 16)], edge_hid.at[pl.ds(16, 16)], to_corner),
+        (tok_ref, halo_tok.at[2], to_corner),
+        (stage_hid.at[pl.ds(0, 16)], edge_hid.at[pl.ds(0, 16)], to_left),
+        (tok_ref, halo_tok.at[1], to_left),
+        (hid_ref.at[pl.ds(0, 128)], halo_hid, to_above),
         (tok_ref, halo_tok.at[0], to_above),
-        (tok_ref, halo_tok.at[1], to_left),
-        (tok_ref, halo_tok.at[2], to_corner),
-        (stage.at[pl.ds(0, 16)], halo_rd.at[pl.ds(0, 16)], to_left),
-        (stage.at[pl.ds(16, 16)], halo_rd.at[pl.ds(16, 16)], to_corner),
-        (hid_ref.at[pl.ds(0, 128)], halo_hid, to_above),
+        (stage_og.at[pl.ds(16, 16)], edge_og.at[pl.ds(16, 16)], to_corner),
+        (stage_og.at[pl.ds(0, 16)], edge_og.at[pl.ds(0, 16)], to_left),
         (og_ref.at[pl.ds(0, 128)], halo_og, to_above),
     ]):
         halo.append(send(src, dst, halo_ss.at[n], halo_rs.at[n], device))
 
+    loads[3].wait()
+    rb = load_rel_bias(rb_ref[...])
     wide_row, wide_lane = iota((128, 512), 0), iota((128, 512), 1)
     pair_sum = jnp.where(
         (wide_row >> 4) == (wide_lane >> 6), (wide_row & 15) + ((wide_lane >> 3) & 7), -1
     )
-    rb = rb_ref[...]
     rb_high = rb.astype(BF)
     rb_rest = rb - rb_high.astype(F32)
     rb_mid = rb_rest.astype(BF)
@@ -173,9 +203,11 @@
     pick_main = one_hot((t_col < 28) & (s_lane == 32 * t_row + t_col + 4))
     e_row, e_col = window_cell(iota((CELLS, 32), 0))
     pick_edge = one_hot((e_col >= 28) & (iota((CELLS, 32), 1) == 4 * e_row + e_col - 28))
-
-    for n in range(6):
-        halo[n].wait_recv()
+    for load in loads[4:]:
+        load.wait()
+
+    for copy in halo[:6]:
+        copy.wait_recv()
     tok = tok_ref[...]
     tok_below, tok_right, tok_corner = halo_tok[0], halo_tok[1], halo_tok[2]
     tok_main = jnp.concatenate(
@@ -196,7 +228,7 @@
         jnp.where(ids < 2.5, emb[2:3], emb[3:4]),
     )
     main_hid = jnp.concatenate([hid_ref[128:256, :], halo_hid[...]], axis=0)
-    resid_in = dot(pick_main, main_hid) + dot(pick_edge, halo_rd[:, :D]) + token_part
+    resid_in = dot(pick_main, main_hid) + dot(pick_edge, edge_hid[...]) + token_part
     normed_one, inv_one = layer_norm(resid_in)
     gain_one = g1_ref[...]
     normal_low = (normed_one * gain_one).astype(BF)
@@ -225,9 +257,10 @@
     gain_two = g2_ref[...]
     mlp_in = (normed_two * gain_two).astype(BF)
 
-    halo[6].wait_recv()
+    for copy in halo[6:]:
+        copy.wait_recv()
     main_og = jnp.concatenate([og_ref[128:256, :], halo_og[...]], axis=0)
-    grad_f32 = dot(pick_main, main_og) + dot(pick_edge, halo_rd[:, D:])
+    grad_f32 = dot(pick_main, main_og) + dot(pick_edge, edge_og[...])
     grad = grad_f32.astype(BF)
 
     grad_mid = jnp.zeros((CELLS, D), F32)
@@ -254,13 +287,11 @@
 
     mlp = dict(
         unit=MLP_UNIT, f32=mlp_f32, send=mlp_send, recv=mlp_recv, x=mlp_x, y=mlp_y, rx=mlp_rx, ry=mlp_ry,
-        x3=mlp_x3, y3=mlp_y3, rx3=mlp_rx3, ry3=mlp_ry3, z=mlp_z, rz=mlp_rz, c=mlp_c, rc=mlp_rc,
-        ss=mlp_ss, rs=mlp_rs, zs=mlp_zs, zr=mlp_zr,
+        ss=mlp_ss, rs=mlp_rs,
     )
     att = dict(
         unit=ATT_UNIT, f32=att_f32, send=att_send, recv=att_recv, x=att_x, y=att_y, rx=att_rx, ry=att_ry,
-        x3=att_x3, y3=att_y3, rx3=att_rx3, ry3=att_ry3, z=att_z, rz=att_rz, c=att_c, rc=att_rc,
-        ss=att_ss, rs=att_rs, zs=att_zs, zr=att_zr,
+        ss=att_ss, rs=att_rs,
     )
     sends = []
 
@@ -273,17 +304,17 @@
         b["p1"][0].wait_recv()
         unit = b["unit"]
         part = NZ_LO // 2 * NY * unit
+        quarter = part // NY
         for x in range(NX):
             first, second = slice(2 * part * x, 2 * part * x + part), slice(2 * part * x + part, 2 * part * (x + 1))
             total = b["f32"][core, first, :] + b["recv"][first, :].astype(F32)
             b["x"][x] = total.astype(BF)
             total = b["f32"][core, second, :] + b["recv"][second, :].astype(F32)
             total = total.reshape(NZ_LO // 2, NY, unit, 128)
-            quarter = part // NY
             for y in range(NY):
                 b["y"][y, quarter * x : quarter * (x + 1), :] = total[:, y].reshape(quarter, 128).astype(BF)
         b["p2"] = []
-        for d in range(1, NX):
+        for d in (2, 1, 3):
             other = (x_at + d) % NX
             b["p2"].append(
                 send(b["x"].at[other], b["rx"].at[d - 1], b["ss"].at[d], b["rs"].at[d], at_x(other))
@@ -294,75 +325,6 @@
             )
         sends.extend(b["p2"])
 
-    def start_yx(b):
-        for copy in b["p2"]:
-            copy.wait_recv()
-        unit = b["unit"]
-        quarter = NZ_LO // 2 * unit
-        total = b["x"][x_at].astype(F32)
-        for d in range(NX - 1):
-            total = total + b["rx"][d].astype(F32)
-        total = total.reshape(NZ_LO // 2, NY, unit, 128)
-        for y in range(NY):
-            b["x3"][y] = total[:, y].reshape(quarter, 128).astype(BF)
-        total = b["y"][y_at].astype(F32)
-        for d in range(NY - 1):
-            total = total + b["ry"][d].astype(F32)
-        for x in range(NX):
-            b["y3"][x] = total[quarter * x : quarter * (x + 1)].astype(BF)
-        b["p3"] = []
-        for d in range(1, NX):
-            other = (y_at + d) % NY
-            b["p3"].append(
-                send(b["x3"].at[other], b["rx3"].at[d - 1], b["ss"].at[6 + d], b["rs"].at[6 + d], at_y(other))
-            )
-            other = (x_at + d) % NX
-            b["p3"].append(
-                send(b["y3"].at[other], b["ry3"].at[d - 1], b["ss"].at[9 + d], b["rs"].at[9 + d], at_x(other))
-            )
-        sends.extend(b["p3"])
-
-    def start_z(b):
-        for copy in b["p3"]:
-            copy.wait_recv()
-        unit = b["unit"]
-        for part, own, own_at, got in ((0, b["x3"], y_at, b["rx3"]), (1, b["y3"], x_at, b["ry3"])):
-            total = own[own_at].astype(F32)
-            for d in range(NX - 1):
-                total = total + got[d].astype(F32)
-            piece = unit // 2
-            for lo in range(NZ_LO // 2):
-                for hi in range(NZ_HI):
-                    start = lo * unit + hi * piece
-                    b["z"][part * (NZ_LO // 2) + lo, hi] = total[start : start + piece]
-        b["p4"] = []
-        for d in range(1, NZ):
-            other = (z_at + d) % NZ
-            b["p4"].append(
-                send(
-                    b["z"].at[other % NZ_LO, other // NZ_LO], b["rz"].at[d - 1],
-                    b["zs"].at[d - 1], b["zr"].at[d - 1], at_z(other),
-                )
-            )
-        sends.extend(b["p4"])
-
-    def start_last(b):
-        for copy in b["p4"]:
-            copy.wait_recv()
-        total = b["z"][z_lo, z_hi]
-        for d in range(NZ - 1):
-            total = total + b["rz"][d]
-        rows = b["unit"] // 4
-        b["c"][0] = total[:rows]
-        b["c"][1] = total[rows:]
-        b["p5"] = [send(b["c"].at[mate], b["rc"], b["ss"].at[13], b["rs"].at[13], at_mate())]
-        sends.extend(b["p5"])
-
-    def finish(b):
-        b["p5"][0].wait_recv()
-        own, got = b["c"][core], b["rc"][...]
-        return jnp.where(core == 0, own, got), jnp.where(core == 0, got, own)
-
     start_mate(mlp)
 
     grad_res = grad_f32 + norm_back(grad_mid, normed_two, inv_two, gain_two)
@@ -372,8 +334,6 @@
     att_f32[1, 768:, :] = proj_grad[:, 128:]
     grad_context = dot_nt(grad_res_low, wproj_ref[...]).astype(BF)
 
-    start_xy(mlp)
-
     grad_probs = jnp.concatenate(
         [dot_nt(grad_context[64 * w : 64 * w + 64], ve_s[w]) for w in range(4)], axis=0
     )
@@ -381,8 +341,6 @@
     grad_scores = probs * (grad_probs - block_sum(probs * grad_probs, ones_pair))
     scores_low = grad_scores.astype(BF)
     probs_low = probs.astype(BF)
-
-    start_yx(mlp)
 
     head_of_lane = iota((64, D), 1) >> 5
 
@@ -398,13 +356,13 @@
         dqkv_s[cells, D : 2 * D] = (own_heads(dot_tn(scores_low[cells], qkv_s[cells, :D])) * SCALE).astype(BF)
         dqkv_s[cells, 2 * D :] = own_heads(dot_tn(probs_low[cells], grad_context[cells])).astype(BF)
 
-    start_z(mlp)
-
     for m in range(3):
         part_grad = dot_tn(normal_low, dqkv_s[:, D * m : D * (m + 1)])
         att_f32[0, pl.ds(m, 256, stride=3), :] = part_grad[:, :128]
         att_f32[1, pl.ds(m, 256, stride=3), :] = part_grad[:, 128:]
+
     start_mate(att)
+    start_xy(mlp)
 
     grad_norm_in = dot_nt(dqkv_s[...], wqkv_ref[...])
     grad_in = (grad_res + norm_back(grad_norm_in, normed_one, inv_one, gain_one)).astype(BF)
@@ -414,17 +372,65 @@
     place_edge = one_hot((v_col >= 28) & (iota((32, CELLS), 0) == 4 * v_row + v_col - 28))
     back_main[...] = dot(place_main, grad_in).astype(BF)
     back_rd[...] = dot(place_edge, grad_in).astype(BF)
+
+    start_xy(att)
+
     to_below, to_right, to_last = (x_at, below, col), (x_at, row, right), (x_at, below, right)
     back = []
     for n, (src, dst, device) in enumerate([
+        (back_rd.at[pl.ds(16, 16)], got_rd.at[pl.ds(16, 16)], to_last),
         (back_rd.at[pl.ds(0, 16)], got_rd.at[pl.ds(0, 16)], to_right),
-        (back_rd.at[pl.ds(16, 16)], got_rd.at[pl.ds(16, 16)], to_last),
         (back_main.at[pl.ds(128, 128)], got_up, to_below),
     ]):
         back.append(send(src, dst, back_ss.at[n], back_rs.at[n], device))
 
-    start_xy(att)
-    start_last(mlp)
+    first_parts, second_parts = [], []
+    for b in (mlp, att):
+        for copy in b["p2"]:
+            copy.wait_recv()
+        total = b["x"][x_at].astype(F32)
+        for d in range(NX - 1):
+            total = total + b["rx"][d].astype(F32)
+        first_parts.append(total.reshape(NZ_LO // 2, NY, b["unit"], 128))
+        total = b["y"][y_at].astype(F32)
+        for d in range(NY - 1):
+            total = total + b["ry"][d].astype(F32)
+        second_parts.append(total.reshape(NX, NZ_LO // 2 * b["unit"], 128))
+    for y in range(NY):
+        x3[y, 0:64, :] = first_parts[0][:, y].reshape(64, 128).astype(BF)
+        x3[y, 64:96, :] = first_parts[1][:, y].reshape(32, 128).astype(BF)
+    for x in range(NX):
+        y3[x, 0:64, :] = second_parts[0][x].astype(BF)
+        y3[x, 64:96, :] = second_parts[1][x].astype(BF)
+    swaps = []
+    for d in (2, 1, 3):
+        other = (y_at + d) % NY
+        swaps.append(send(x3.at[other], rx3.at[d - 1], late_ss.at[d - 1], late_rs.at[d - 1], at_y(other)))
+        other = (x_at + d) % NX
+        swaps.append(send(y3.at[other], ry3.at[d - 1], late_ss.at[2 + d], late_rs.at[2 + d], at_x(other)))
+
+    for copy in swaps:
+        copy.wait_recv()
+    for part, own, own_at, got in ((0, x3, y_at, rx3), (1, y3, x_at, ry3)):
+        total = own[own_at].astype(F32)
+        for d in range(NX - 1):
+            total = total + got[d].astype(F32)
+        for lo in range(NZ_LO // 2):
+            for hi in range(NZ_HI):
+                at_mlp, at_att = 16 * lo + 8 * hi, 64 + 8 * lo + 4 * hi
+                piece = jnp.concatenate(
+                    [total[at_mlp : at_mlp + 8], total[at_att : at_att + 4], jnp.zeros((4, 128), F32)], axis=0
+                )
+                z_send[part * (NZ_LO // 2) + lo, hi] = piece.astype(BF)
+    ring = []
+    for d in (8, 7, 9, 6, 10, 5, 11, 4, 12, 3, 13, 2, 14, 1, 15):
+        other = (z_at + d) % NZ
+        ring.append(
+            send(
+                z_send.at[other % NZ_LO, other // NZ_LO], z_recv.at[d - 1],
+                z_ss.at[d - 1], z_rs.at[d - 1], at_z(other),
+            )
+        )
 
     for copy in back:
         copy.wait_recv()
@@ -432,24 +438,31 @@
     out_ref[0:128, :] = (got_up[...].astype(F32) + dot(spread, got_rd[16:32, :])).astype(BF)
     out_ref[128:256, :] = (back_main[0:128, :].astype(F32) + dot(spread, got_rd[0:16, :])).astype(BF)
 
-    start_yx(att)
-    start_z(att)
-    first, second = finish(mlp)
-    apart = jnp.concatenate([first, second], axis=0)
+    for copy in ring:
+        copy.wait_recv()
+    total = z_send[z_lo, z_hi].astype(F32)
+    for d in range(NZ - 1):
+        total = total + z_recv[d].astype(F32)
+    for k in range(2):
+        c_send[k] = jnp.concatenate(
+            [total[4 * k : 4 * k + 4], total[8 + 2 * k : 10 + 2 * k], total[12:14]], axis=0
+        )
+    last = send(c_send.at[mate], c_recv, late_ss.at[6], late_rs.at[6], at_mate())
+    last.wait_recv()
+    own, got = c_send[core], c_recv[...]
+    first, second = jnp.where(core == 0, own, got), jnp.where(core == 0, got, own)
+    apart = jnp.concatenate([first[0:4], second[0:4]], axis=0)
     mixed = jnp.concatenate([part[i : i + 1] for i in range(4) for part in (first, second)], axis=0)
     mlp_ref[...] = jnp.where(x_at < 2, apart, mixed)
-
-    start_last(att)
-    first, second = finish(att)
-    att_ref[...] = jnp.concatenate([first[0:1], second[0:1], first[1:2], second[1:2]], axis=0)
-
-    for copy in halo + back + sends:
+    att_ref[...] = jnp.concatenate([first[4:5], second[4:5], first[5:6], second[5:6]], axis=0)
+
+    for copy in halo + back + sends + swaps + ring + [last]:
         copy.wait_send()
 
 
 def reduce_scratch(unit):
     chip_rows = NZ_LO * NY * unit
-    half, quarter = chip_rows // 2, chip_rows // 8
+    half = chip_rows // 2
     return [
         pltpu.VMEM((2, NX * chip_rows, 128), F32),
         pltpu.VMEM((NX * chip_rows, 128), BF),
@@ -458,23 +471,27 @@
         pltpu.VMEM((NY, half, 128), BF),
         pltpu.VMEM((NX - 1, half, 128), BF),
         pltpu.VMEM((NY - 1, half, 128), BF),
-        pltpu.VMEM((NY, quarter, 128), BF),
-        pltpu.VMEM((NX, quarter, 128), BF),
-        pltpu.VMEM((NY - 1, quarter, 128), BF),
-        pltpu.VMEM((NX - 1, quarter, 128), BF),
-        pltpu.VMEM((NZ_LO, NZ_HI, unit // 2, 128), F32),
-        pltpu.VMEM((NZ - 1, unit // 2, 128), F32),
-        pltpu.VMEM((2, unit // 4, 128), F32),
-        pltpu.VMEM((unit // 4, 128), F32),
     ]
 
 
 def on_device(
     hidden_in, token_ids, embed, norm1_gain, norm2_gain, w_qkv, rel_bias, w_proj, w_up, w_down, out_grad
 ):
-    table = rel_bias.reshape(HEADS, 15, 15).transpose(1, 0, 2)
-    table = jnp.pad(table, ((0, 1), (0, 0), (0, 1))).reshape(16, 128)
     dma = pltpu.SemaphoreType.DMA
+    operands = (
+        hidden_in.reshape(CELLS, D),
+        token_ids.reshape(8, 32),
+        embed,
+        norm1_gain.reshape(1, D),
+        norm2_gain.reshape(1, D),
+        w_qkv,
+        rel_bias,
+        w_proj,
+        w_up,
+        w_down,
+        out_grad.reshape(CELLS, D),
+    )
+    chunk = NZ_LO // 2 * (MLP_UNIT + ATT_UNIT)
     grad_out, attention_grads, mlp_grads = pl.pallas_call(
         kernel,
         out_shape=(
@@ -482,13 +499,16 @@
             jax.ShapeDtypeStruct((4, 128), F32),
             jax.ShapeDtypeStruct((8, 128), F32),
         ),
-        in_specs=[pl.BlockSpec(memory_space=pltpu.VMEM)] * 11,
+        in_specs=[pl.BlockSpec(memory_space=pltpu.HBM)] * len(operands),
         out_specs=[pl.BlockSpec(memory_space=pltpu.VMEM)] * 3,
-        scratch_shapes=[
-            pltpu.VMEM((32, 2 * D), BF),
+        scratch_shapes=[pltpu.VMEM(operand.shape, operand.dtype) for operand in operands]
+        + [
+            pltpu.VMEM((32, D), BF),
+            pltpu.VMEM((32, D), BF),
             pltpu.VMEM((128, D), BF),
             pltpu.VMEM((128, D), BF),
-            pltpu.VMEM((32, 2 * D), BF),
+            pltpu.VMEM((32, D), BF),
+            pltpu.VMEM((32, D), BF),
             pltpu.VMEM((3, 8, 32), jnp.int32),
             pltpu.VMEM((64, 512), F32),
             pltpu.VMEM((CELLS, 512), F32),
@@ -496,8 +516,6 @@
             pltpu.VMEM((4, 512, D), BF),
             pltpu.VMEM((CELLS, 3 * D), BF),
             pltpu.VMEM((CELLS, D), BF),
-            pltpu.VMEM((CELLS, FF), BF),
-            pltpu.VMEM((CELLS, FF), BF),
             pltpu.VMEM((CELLS, 3 * D), BF),
             pltpu.VMEM((CELLS, D), BF),
             pltpu.VMEM((32, D), BF),
@@ -506,25 +524,24 @@
         ]
         + reduce_scratch(MLP_UNIT)
         + reduce_scratch(ATT_UNIT)
-        + [dma((7,)), dma((7,)), dma((3,)), dma((3,)), dma((14,)), dma((14,)), dma((14,)), dma((14,))]
-        + [dma((NZ - 1,))] * 4,
+        + [
+            pltpu.VMEM((NY, chunk, 128), BF),
+            pltpu.VMEM((NX, chunk, 128), BF),
+            pltpu.VMEM((NY - 1, chunk, 128), BF),
+            pltpu.VMEM((NX - 1, chunk, 128), BF),
+            pltpu.VMEM((NZ_LO, NZ_HI, 16, 128), BF),
+            pltpu.VMEM((NZ - 1, 16, 128), BF),
+            pltpu.VMEM((2, 8, 128), F32),
+            pltpu.VMEM((8, 128), F32),
+        ]
+        + [dma((len(operands),)), dma((9,)), dma((9,)), dma((3,)), dma((3,))]
+        + [dma((7,))] * 6
+        + [dma((NZ - 1,))] * 2,
         compiler_params=pltpu.CompilerParams(
-            collective_id=0, has_side_effects=True, vmem_limit_bytes=48 * 1024 * 1024
+            collective_id=0, has_side_effects=True, vmem_limit_bytes=62 * 1024 * 1024
         ),
         name="decoder_block_backward",
-    )(
-        hidden_in.reshape(CELLS, D),
-        token_ids.reshape(8, 32),
-        embed,
-        norm1_gain.reshape(1, D),
-        norm2_gain.reshape(1, D),
-        w_qkv,
-        table,
-        w_proj,
-        w_up,
-        w_down,
-        out_grad.reshape(CELLS, D),
-    )
+    )(*operands)
     return grad_out.reshape(1, 8, 32, D), attention_grads, mlp_grads
 
 

time: 75.6 us -> 57.5 us (0.76)
  Pallas kernels: 66.4 us -> 53.9 us
  local copies, waits for them, and re-layouts: 8.14 us -> 2.84 us
    pallas_call x1, Pallas kernels: 66.4 us -> 53.9 us  [on_device(): pl.pallas_call(kernel, out_shape=(jax.ShapeDtypeStruct((CELLS, D), BF), j...]
    unnamed x26 -> x7, local copies, waits for them, and re-layouts: 7.97 us -> 2.84 us
where the time goes in v2:
time: 57.5 us; the launch traced here: 57.4 us
  Pallas kernels  53.9 us (94%)
  local copies, waits for them, and re-layouts  2.84 us (5%)
  between operations  0.65 us (1%)
    pallas_call x1, Pallas kernels, on_device(): pl.pallas_call(kernel, out_shape=(jax.ShapeDtypeStruct((CELLS, D), BF), j...  53.9 us
    unnamed x7, local copies, waits for them, and re-layouts  2.84 us

profile of v2, /device:TPU:1, one launch (start us, length us, event | category | flops | bytes accessed | tf_op | source)
XLA Modules:
  0.0 57.4 jit_solution(3838198171804781070)
XLA Ops:
  0.6 53.9 %decoder_block_backward.1 = (bf16[256,256]{1,0:T(8,128)(2,1)}, f32[4,128]{1,0:T(4,128)}, f32[8,128]{1,0:T(8,128)}) custom-call(bf16[256,256]{1,0:T(8,128)(2,1)} %bitcast.6, s32[8,32]{1,0:T(8,128)} %bitcast.9, bf16[4,256]{1,0:T(4,128)(2,1)} %emb_in.1, f32[1,256]{1,0:T(1,128)} %bitcast.10, f32[1,256]{1,0:T(1,128)} %bitcast.11, bf16[256,768]{1,0:T(8,128)(2,1)} %wqkv_in.1, ...), custom_call_target="tpu_custom_call" | custom-call | tf_op jit(solution)/shard_map/decoder_block_backward/pallas_call | solution.py:495
  54.5 0.0 copy-start.1
  54.5 1.6 %copy.17 = bf16[1,8,32,256]{3,2,1,0:T(8,128)(2,1)} copy(bf16[1,8,32,256]{3,2,1,0:T(8,128)(2,1)} %bitcast.8) | data formatting | bytes 262144
  56.1 0.0 copy-done.1
  56.1 0.0 copy-start
  56.1 0.6 %copy.18 = f32[4,128]{1,0:T(4,128)} copy(f32[4,128]{1,0:T(4,128)S(1)} %copy-done.1) | data formatting | bytes 4096
  56.7 0.1 copy-done
  56.8 0.6 %copy.19 = f32[8,128]{1,0:T(8,128)} copy(f32[8,128]{1,0:T(8,128)S(1)} %copy-done) | data formatting | bytes 8192
Async XLA Ops:
  54.5 1.6 %copy-start.1 = (f32[4,128]{1,0:T(4,128)S(1)}, f32[4,128]{1,0:T(4,128)}, u32[]{:S(2)}) copy-start(f32[4,128]{1,0:T(4,128)} %get-tuple-element.13) | copy-start | bytes 6148
  56.1 0.7 %copy-start = (f32[8,128]{1,0:T(8,128)S(1)}, f32[8,128]{1,0:T(8,128)}, u32[]{:S(2)}) copy-start(f32[8,128]{1,0:T(8,128)} %get-tuple-element.14) | copy-start | bytes 12292

commit v3 on v2

--- a/solution.py
+++ b/solution.py
@@ -100,7 +100,7 @@
     mlp_f32, mlp_send, mlp_recv, mlp_x, mlp_y, mlp_rx, mlp_ry,
     att_f32, att_send, att_recv, att_x, att_y, att_rx, att_ry,
     x3, y3, rx3, ry3, z_send, z_recv, c_send, c_recv,
-    in_sem, halo_ss, halo_rs, back_ss, back_rs, mlp_ss, mlp_rs, att_ss, att_rs, late_ss, late_rs, z_ss, z_rs,
+    in_sem, halo_ss, halo_rs, back_ss, back_rs, mlp_ss, mlp_rs, att_ss, att_rs, late_ss, late_rs, z_ss, z_rs, ring_sem,
 ):
     loads = [
         pltpu.make_async_copy(src, dst, in_sem.at[n])
@@ -136,14 +136,20 @@
     def at_z(other):
         return (x_at, (other % NZ_LO) * NY + y_at, (other // NZ_LO) * 2 + core)
 
-    partners = [(x_at, above, left), (x_at, below, right), (x_at, above, col), (x_at, below, col)]
-    partners += [(x_at, row, left), (x_at, row, right), at_mate()]
-    partners += [at_x((x_at + d) % NX) for d in range(1, NX)]
-    partners += [at_y((y_at + d) % NY) for d in range(1, NY)]
-    partners += [at_z((z_at + d) % NZ) for d in range(1, NZ)]
     barrier = pltpu.get_barrier_semaphore()
-    for partner in partners:
+    near = [at_mate()]
+    near += [at_x((x_at + d) % NX) for d in range(1, NX)]
+    near += [at_y((y_at + d) % NY) for d in range(1, NY)]
+    near += [at_z((z_at + 1) % NZ), at_z((z_at + NZ - 1) % NZ)]
+    for partner in [(x_at, below, right), (x_at, below, col), (x_at, row, right)] + near:
         pl.semaphore_signal(barrier, inc=1, device_id=partner, device_id_type=MESH)
+
+    def spread_ring(n):
+        for other in ((z_at + 2**n) % NZ, (z_at + NZ - 2**n) % NZ):
+            pl.semaphore_signal(ring_sem.at[n], inc=1, device_id=at_z(other), device_id_type=MESH)
+
+    def hear_ring(n):
+        pl.semaphore_wait(ring_sem.at[n], 2)
 
     def send(src, dst, send_sem, recv_sem, device):
         copy = pltpu.make_async_remote_copy(
@@ -161,7 +167,7 @@
     stage_hid[...] = dot(pick, hid_ref[...]).astype(BF)
     stage_og[...] = dot(pick, og_ref[...]).astype(BF)
 
-    pl.semaphore_wait(barrier, len(partners))
+    pl.semaphore_wait(barrier, 3 + len(near))
 
     to_above, to_left, to_corner = (x_at, above, col), (x_at, row, left), (x_at, above, left)
     halo = []
@@ -177,6 +183,8 @@
         (og_ref.at[pl.ds(0, 128)], halo_og, to_above),
     ]):
         halo.append(send(src, dst, halo_ss.at[n], halo_rs.at[n], device))
+
+    spread_ring(0)
 
     loads[3].wait()
     rb = load_rel_bias(rb_ref[...])
@@ -326,6 +334,8 @@
         sends.extend(b["p2"])
 
     start_mate(mlp)
+    hear_ring(0)
+    spread_ring(1)
 
     grad_res = grad_f32 + norm_back(grad_mid, normed_two, inv_two, gain_two)
     grad_res_low = grad_res.astype(BF)
@@ -374,6 +384,8 @@
     back_rd[...] = dot(place_edge, grad_in).astype(BF)
 
     start_xy(att)
+    hear_ring(1)
+    spread_ring(2)
 
     to_below, to_right, to_last = (x_at, below, col), (x_at, row, right), (x_at, below, right)
     back = []
@@ -411,6 +423,7 @@
 
     for copy in swaps:
         copy.wait_recv()
+    hear_ring(2)
     for part, own, own_at, got in ((0, x3, y_at, rx3), (1, y3, x_at, ry3)):
         total = own[own_at].astype(F32)
         for d in range(NX - 1):
@@ -536,7 +549,8 @@
         ]
         + [dma((len(operands),)), dma((9,)), dma((9,)), dma((3,)), dma((3,))]
         + [dma((7,))] * 6
-        + [dma((NZ - 1,))] * 2,
+        + [dma((NZ - 1,))] * 2
+        + [pltpu.SemaphoreType.REGULAR((3,))],
         compiler_params=pltpu.CompilerParams(
             collective_id=0, has_side_effects=True, vmem_limit_bytes=62 * 1024 * 1024
         ),

time: 57.5 us -> 57.4 us (level)
  no operation moved by 1% of the time
where the time goes in v3:
time: 57.4 us; the launch traced here: 57.2 us
  Pallas kernels  53.7 us (94%)
  local copies, waits for them, and re-layouts  2.84 us (5%)
  between operations  0.65 us (1%)
    pallas_call x1, Pallas kernels, on_device(): pl.pallas_call(kernel, out_shape=(jax.ShapeDtypeStruct((CELLS, D), BF), j...  53.7 us
    unnamed x7, local copies, waits for them, and re-layouts  2.84 us

profile of v3, /device:TPU:1, one launch (start us, length us, event | category | flops | bytes accessed | tf_op | source)
XLA Modules:
  0.0 57.2 jit_solution(2336257565250695113)
XLA Ops:
  0.6 53.7 %decoder_block_backward.1 = (bf16[256,256]{1,0:T(8,128)(2,1)}, f32[4,128]{1,0:T(4,128)}, f32[8,128]{1,0:T(8,128)}) custom-call(bf16[256,256]{1,0:T(8,128)(2,1)} %bitcast.6, s32[8,32]{1,0:T(8,128)} %bitcast.9, bf16[4,256]{1,0:T(4,128)(2,1)} %emb_in.1, f32[1,256]{1,0:T(1,128)} %bitcast.10, f32[1,256]{1,0:T(1,128)} %bitcast.11, bf16[256,768]{1,0:T(8,128)(2,1)} %wqkv_in.1, ...), custom_call_target="tpu_custom_call" | custom-call | tf_op jit(solution)/shard_map/decoder_block_backward/pallas_call | solution.py:508
  54.3 0.0 copy-start.1
  54.3 1.6 %copy.17 = bf16[1,8,32,256]{3,2,1,0:T(8,128)(2,1)} copy(bf16[1,8,32,256]{3,2,1,0:T(8,128)(2,1)} %bitcast.8) | data formatting | bytes 262144
  55.9 0.0 copy-done.1
  55.9 0.0 copy-start
  55.9 0.6 %copy.18 = f32[4,128]{1,0:T(4,128)} copy(f32[4,128]{1,0:T(4,128)S(1)} %copy-done.1) | data formatting | bytes 4096
  56.5 0.1 copy-done
  56.6 0.6 %copy.19 = f32[8,128]{1,0:T(8,128)} copy(f32[8,128]{1,0:T(8,128)S(1)} %copy-done) | data formatting | bytes 8192
Async XLA Ops:
  54.3 1.6 %copy-start.1 = (f32[4,128]{1,0:T(4,128)S(1)}, f32[4,128]{1,0:T(4,128)}, u32[]{:S(2)}) copy-start(f32[4,128]{1,0:T(4,128)} %get-tuple-element.13) | copy-start | bytes 6148
  55.9 0.7 %copy-start = (f32[8,128]{1,0:T(8,128)S(1)}, f32[8,128]{1,0:T(8,128)}, u32[]{:S(2)}) copy-start(f32[8,128]{1,0:T(8,128)} %get-tuple-element.14) | copy-start | bytes 12292

commit v4 on v3

--- a/solution.py
+++ b/solution.py
@@ -100,7 +100,7 @@
     mlp_f32, mlp_send, mlp_recv, mlp_x, mlp_y, mlp_rx, mlp_ry,
     att_f32, att_send, att_recv, att_x, att_y, att_rx, att_ry,
     x3, y3, rx3, ry3, z_send, z_recv, c_send, c_recv,
-    in_sem, halo_ss, halo_rs, back_ss, back_rs, mlp_ss, mlp_rs, att_ss, att_rs, late_ss, late_rs, z_ss, z_rs, ring_sem,
+    in_sem, halo_ss, halo_rs, back_ss, back_rs, mlp_ss, mlp_rs, att_ss, att_rs, late_ss, late_rs, z_ss, z_rs, ring_sem, pass_ss, go_sem,
 ):
     loads = [
         pltpu.make_async_copy(src, dst, in_sem.at[n])
@@ -136,13 +136,63 @@
     def at_z(other):
         return (x_at, (other % NZ_LO) * NY + y_at, (other // NZ_LO) * 2 + core)
 
+    row_first = 1 - (row + ROW_DEVICES - 1) // ROW_DEVICES
+    col_first = 1 - (col + COL_DEVICES - 1) // COL_DEVICES
+    row_last, col_last = row == ROW_DEVICES - 1, col == COL_DEVICES - 1
+    half_way = ROW_DEVICES // 2
+    relay = (x_at, (row + half_way) % ROW_DEVICES, 0)
+    is_relay = col == 0
+    post = (x_at, half_way + col, 1)
+    post_col = row - half_way
+    is_post = jnp.logical_and(col == 1, jnp.logical_and(row >= half_way, row < half_way + COL_DEVICES))
+    is_corner_post = jnp.logical_and(is_post, row % 2 == 1)
+    corner_by_post = jnp.logical_and(row_last, core == 0)
+    mail_corner = 1 - (1 - col_first) * (1 - row_first * core)
+    far_left = (x_at, relay[1], COL_DEVICES - 1)
+    far_corner = (x_at, (relay[1] + ROW_DEVICES - 1) % ROW_DEVICES, COL_DEVICES - 1)
+    far_above = (x_at, ROW_DEVICES - 1, post_col)
+    far_above_left = (x_at, ROW_DEVICES - 1, (post_col + COL_DEVICES - 1) % COL_DEVICES)
+
     barrier = pltpu.get_barrier_semaphore()
+
+    def enter(*device):
+        pl.semaphore_signal(barrier, inc=1, device_id=device, device_id_type=MESH)
+
+    @pl.when(is_relay)
+    def _():
+        enter(*relay)
+        enter(*relay)
+        enter(*far_left)
+        enter(*far_corner)
+
+    @pl.when(is_post)
+    def _():
+        enter(x_at, 0, post_col)
+        enter(*far_above)
+
+    @pl.when(is_corner_post)
+    def _():
+        enter(x_at, 0, post_col)
+        enter(*far_above_left)
+
+    @pl.when(jnp.logical_not(row_last))
+    def _():
+        enter(x_at, below, col)
+
+    @pl.when(jnp.logical_not(col_last))
+    def _():
+        enter(x_at, row, right)
+
+    @pl.when(jnp.logical_not(jnp.logical_or(col_last, corner_by_post)))
+    def _():
+        enter(x_at, below, right)
+
     near = [at_mate()]
     near += [at_x((x_at + d) % NX) for d in range(1, NX)]
     near += [at_y((y_at + d) % NY) for d in range(1, NY)]
     near += [at_z((z_at + 1) % NZ), at_z((z_at + NZ - 1) % NZ)]
-    for partner in [(x_at, below, right), (x_at, below, col), (x_at, row, right)] + near:
-        pl.semaphore_signal(barrier, inc=1, device_id=partner, device_id_type=MESH)
+    for partner in near:
+        enter(*partner)
 
     def spread_ring(n):
         for other in ((z_at + 2**n) % NZ, (z_at + NZ - 2**n) % NZ):
@@ -167,22 +217,69 @@
     stage_hid[...] = dot(pick, hid_ref[...]).astype(BF)
     stage_og[...] = dot(pick, og_ref[...]).astype(BF)
 
-    pl.semaphore_wait(barrier, 3 + len(near))
-
-    to_above, to_left, to_corner = (x_at, above, col), (x_at, row, left), (x_at, above, left)
-    halo = []
-    for n, (src, dst, device) in enumerate([
-        (stage_hid.at[pl.ds(16, 16)], edge_hid.at[pl.ds(16, 16)], to_corner),
-        (tok_ref, halo_tok.at[2], to_corner),
-        (stage_hid.at[pl.ds(0, 16)], edge_hid.at[pl.ds(0, 16)], to_left),
-        (tok_ref, halo_tok.at[1], to_left),
-        (hid_ref.at[pl.ds(0, 128)], halo_hid, to_above),
-        (tok_ref, halo_tok.at[0], to_above),
-        (stage_og.at[pl.ds(16, 16)], edge_og.at[pl.ds(16, 16)], to_corner),
-        (stage_og.at[pl.ds(0, 16)], edge_og.at[pl.ds(0, 16)], to_left),
-        (og_ref.at[pl.ds(0, 128)], halo_og, to_above),
-    ]):
-        halo.append(send(src, dst, halo_ss.at[n], halo_rs.at[n], device))
+    row_end, col_end = (row + 1) // ROW_DEVICES, (col + 1) // COL_DEVICES
+    pl.semaphore_wait(barrier, 3 + len(near) + 2 * col_end + row_end + row_end * (1 - core))
+
+    def go(*device):
+        pl.semaphore_signal(go_sem, inc=1, device_id=device, device_id_type=MESH)
+
+    @pl.when(col_last)
+    def _():
+        go(x_at, (row + half_way) % ROW_DEVICES, 0)
+        go(x_at, (row + 1 + half_way) % ROW_DEVICES, 0)
+
+    @pl.when(row_last)
+    def _():
+        go(*post)
+
+    @pl.when(corner_by_post)
+    def _():
+        go(x_at, half_way + right, 1)
+
+    def blend(flag, one, other):
+        return tuple(flag * a + (1 - flag) * b for a, b in zip(one, other))
+
+    to_above = blend(row_first, post, (x_at, above, col))
+    to_left = blend(col_first, relay, (x_at, row, left))
+    to_corner = blend(col_first, relay, blend(row_first * core, post, (x_at, above, left)))
+    corner, edge = pl.ds(16, 16), pl.ds(0, 16)
+    messages = [
+        (stage_hid.at[corner], lambda k: edge_hid.at[k, corner], mail_corner, to_corner),
+        (tok_ref, lambda k: halo_tok.at[k, 2], mail_corner, to_corner),
+        (stage_hid.at[edge], lambda k: edge_hid.at[k, edge], col_first, to_left),
+        (tok_ref, lambda k: halo_tok.at[k, 1], col_first, to_left),
+        (hid_ref.at[pl.ds(0, 128)], lambda k: halo_hid.at[k], row_first, to_above),
+        (tok_ref, lambda k: halo_tok.at[k, 0], row_first, to_above),
+        (stage_og.at[corner], lambda k: edge_og.at[k, corner], mail_corner, to_corner),
+        (stage_og.at[edge], lambda k: edge_og.at[k, edge], col_first, to_left),
+        (og_ref.at[pl.ds(0, 128)], lambda k: halo_og.at[k], row_first, to_above),
+    ]
+    halo = [
+        send(src, dst(mail), halo_ss.at[n], halo_rs.at[len(messages) * mail + n], device)
+        for n, (src, dst, mail, device) in enumerate(messages)
+    ]
+
+    def passing(n, device):
+        dst = messages[n][1]
+        return pltpu.make_async_remote_copy(
+            src_ref=dst(1), dst_ref=dst(0), send_sem=pass_ss.at[n], recv_sem=halo_rs.at[n],
+            device_id=device, device_id_type=MESH,
+        )
+
+    def arrived(n, k):
+        dst = messages[n][1]
+        pltpu.make_async_remote_copy(
+            src_ref=dst(k), dst_ref=dst(k), send_sem=pass_ss.at[n], recv_sem=halo_rs.at[len(messages) * k + n],
+            device_id=at_mate(), device_id_type=MESH,
+        ).wait_recv()
+
+    passes = [
+        (is_relay, 2, [(0, far_corner), (1, far_corner), (2, far_left), (3, far_left), (6, far_corner), (7, far_left)]),
+        (is_post, 1 + row % 2, []),
+        (is_corner_post, None, [(0, far_above_left), (1, far_above_left)]),
+        (is_post, None, [(4, far_above), (5, far_above), (8, far_above)]),
+        (is_corner_post, None, [(6, far_above_left)]),
+    ]
 
     spread_ring(0)
 
@@ -214,10 +311,20 @@
     for load in loads[4:]:
         load.wait()
 
-    for copy in halo[:6]:
-        copy.wait_recv()
+    for condition, signals, steps in passes:
+
+        @pl.when(condition)
+        def _():
+            if signals is not None:
+                pl.semaphore_wait(go_sem, signals)
+            for n, device in steps:
+                arrived(n, 1)
+                passing(n, device).start()
+
+    for n in range(6):
+        arrived(n, 0)
     tok = tok_ref[...]
-    tok_below, tok_right, tok_corner = halo_tok[0], halo_tok[1], halo_tok[2]
+    tok_below, tok_right, tok_corner = halo_tok[0, 0], halo_tok[0, 1], halo_tok[0, 2]
     tok_main = jnp.concatenate(
         [tok[4 + i : 5 + i, :] for i in range(4)] + [tok_below[i : i + 1, :] for i in range(4)], axis=1
     )
@@ -235,8 +342,8 @@
         jnp.where(ids < 0.5, emb[0:1], emb[1:2]),
         jnp.where(ids < 2.5, emb[2:3], emb[3:4]),
     )
-    main_hid = jnp.concatenate([hid_ref[128:256, :], halo_hid[...]], axis=0)
-    resid_in = dot(pick_main, main_hid) + dot(pick_edge, edge_hid[...]) + token_part
+    main_hid = jnp.concatenate([hid_ref[128:256, :], halo_hid[0]], axis=0)
+    resid_in = dot(pick_main, main_hid) + dot(pick_edge, edge_hid[0]) + token_part
     normed_one, inv_one = layer_norm(resid_in)
     gain_one = g1_ref[...]
     normal_low = (normed_one * gain_one).astype(BF)
@@ -265,10 +372,10 @@
     gain_two = g2_ref[...]
     mlp_in = (normed_two * gain_two).astype(BF)
 
-    for copy in halo[6:]:
-        copy.wait_recv()
-    main_og = jnp.concatenate([og_ref[128:256, :], halo_og[...]], axis=0)
-    grad_f32 = dot(pick_main, main_og) + dot(pick_edge, edge_og[...])
+    for n in range(6, 9):
+        arrived(n, 0)
+    main_og = jnp.concatenate([og_ref[128:256, :], halo_og[0]], axis=0)
+    grad_f32 = dot(pick_main, main_og) + dot(pick_edge, edge_og[0])
     grad = grad_f32.astype(BF)
 
     grad_mid = jnp.zeros((CELLS, D), F32)
@@ -471,6 +578,12 @@
 
     for copy in halo + back + sends + swaps + ring + [last]:
         copy.wait_send()
+    for condition, _, steps in passes:
+
+        @pl.when(condition)
+        def _():
+            for n, device in steps:
+                passing(n, device).wait_send()
 
 
 def reduce_scratch(unit):
@@ -518,11 +631,11 @@
         + [
             pltpu.VMEM((32, D), BF),
             pltpu.VMEM((32, D), BF),
-            pltpu.VMEM((128, D), BF),
-            pltpu.VMEM((128, D), BF),
-            pltpu.VMEM((32, D), BF),
-            pltpu.VMEM((32, D), BF),
-            pltpu.VMEM((3, 8, 32), jnp.int32),
+            pltpu.VMEM((2, 128, D), BF),
+            pltpu.VMEM((2, 128, D), BF),
+            pltpu.VMEM((2, 32, D), BF),
+            pltpu.VMEM((2, 32, D), BF),
+            pltpu.VMEM((2, 3, 8, 32), jnp.int32),
             pltpu.VMEM((64, 512), F32),
             pltpu.VMEM((CELLS, 512), F32),
             pltpu.VMEM((4, 512, D), BF),
@@ -547,10 +660,10 @@
             pltpu.VMEM((2, 8, 128), F32),
             pltpu.VMEM((8, 128), F32),
         ]
-        + [dma((len(operands),)), dma((9,)), dma((9,)), dma((3,)), dma((3,))]
+        + [dma((len(operands),)), dma((9,)), dma((18,)), dma((3,)), dma((3,))]
         + [dma((7,))] * 6
         + [dma((NZ - 1,))] * 2
-        + [pltpu.SemaphoreType.REGULAR((3,))],
+        + [pltpu.SemaphoreType.REGULAR((3,)), dma((9,)), pltpu.SemaphoreType.REGULAR],
         compiler_params=pltpu.CompilerParams(
             collective_id=0, has_side_effects=True, vmem_limit_bytes=62 * 1024 * 1024
         ),

time: 57.4 us -> 55.1 us (0.960)
  Pallas kernels: 53.7 us -> 51.5 us
    pallas_call x1, Pallas kernels: 53.7 us -> 51.5 us  [on_device(): pl.pallas_call(kernel, out_shape=(jax.ShapeDtypeStruct((CELLS, D), BF), j...]
where the time goes in v4:
time: 55.1 us; the launch traced here: 55 us
  Pallas kernels  51.5 us (93%)
  local copies, waits for them, and re-layouts  2.84 us (5%)
  between operations  0.65 us (1%)
    pallas_call x1, Pallas kernels, on_device(): pl.pallas_call(kernel, out_shape=(jax.ShapeDtypeStruct((CELLS, D), BF), j...  51.5 us
    unnamed x7, local copies, waits for them, and re-layouts  2.84 us

profile of v4, /device:TPU:1, one launch (start us, length us, event | category | flops | bytes accessed | tf_op | source)
XLA Modules:
  0.0 55.0 jit_solution(15862601574827516776)
XLA Ops:
  0.6 51.5 %decoder_block_backward.1 = (bf16[256,256]{1,0:T(8,128)(2,1)}, f32[4,128]{1,0:T(4,128)}, f32[8,128]{1,0:T(8,128)}) custom-call(bf16[256,256]{1,0:T(8,128)(2,1)} %bitcast.6, s32[8,32]{1,0:T(8,128)} %bitcast.9, bf16[4,256]{1,0:T(4,128)(2,1)} %emb_in.1, f32[1,256]{1,0:T(1,128)} %bitcast.10, f32[1,256]{1,0:T(1,128)} %bitcast.11, bf16[256,768]{1,0:T(8,128)(2,1)} %wqkv_in.1, ...), custom_call_target="tpu_custom_call" | custom-call | tf_op jit(solution)/shard_map/decoder_block_backward/pallas_call | solution.py:621
  52.1 0.0 copy-start.1
  52.1 1.6 %copy.17 = bf16[1,8,32,256]{3,2,1,0:T(8,128)(2,1)} copy(bf16[1,8,32,256]{3,2,1,0:T(8,128)(2,1)} %bitcast.8) | data formatting | bytes 262144
  53.7 0.0 copy-done.1
  53.7 0.0 copy-start
  53.7 0.6 %copy.18 = f32[4,128]{1,0:T(4,128)} copy(f32[4,128]{1,0:T(4,128)S(1)} %copy-done.1) | data formatting | bytes 4096
  54.3 0.1 copy-done
  54.4 0.6 %copy.19 = f32[8,128]{1,0:T(8,128)} copy(f32[8,128]{1,0:T(8,128)S(1)} %copy-done) | data formatting | bytes 8192
Async XLA Ops:
  52.1 1.6 %copy-start.1 = (f32[4,128]{1,0:T(4,128)S(1)}, f32[4,128]{1,0:T(4,128)}, u32[]{:S(2)}) copy-start(f32[4,128]{1,0:T(4,128)} %get-tuple-element.13) | copy-start | bytes 6148
  53.7 0.7 %copy-start = (f32[8,128]{1,0:T(8,128)S(1)}, f32[8,128]{1,0:T(8,128)}, u32[]{:S(2)}) copy-start(f32[8,128]{1,0:T(8,128)} %get-tuple-element.14) | copy-start | bytes 12292

commit v5 on v4

--- a/solution.py
+++ b/solution.py
@@ -102,6 +102,88 @@
     x3, y3, rx3, ry3, z_send, z_recv, c_send, c_recv,
     in_sem, halo_ss, halo_rs, back_ss, back_rs, mlp_ss, mlp_rs, att_ss, att_rs, late_ss, late_rs, z_ss, z_rs, ring_sem, pass_ss, go_sem,
 ):
+    x_at, row, col = lax.axis_index("dp"), lax.axis_index("row"), lax.axis_index("col")
+    z_lo, y_at = row // NY, row % NY
+    z_hi, core = col // 2, col % 2
+    z_at = z_hi * NZ_LO + z_lo
+    mate = 1 - core
+
+    above = (row + ROW_DEVICES - 1) % ROW_DEVICES
+    below = (row + 1) % ROW_DEVICES
+    left = (col + COL_DEVICES - 1) % COL_DEVICES
+    right = (col + 1) % COL_DEVICES
+
+    def at_mate():
+        return (x_at, row, z_hi * 2 + mate)
+
+    def at_x(other):
+        return (other, row, col)
+
+    def at_y(other):
+        return (x_at, z_lo * NY + other, col)
+
+    def at_z(other):
+        return (x_at, (other % NZ_LO) * NY + y_at, (other // NZ_LO) * 2 + core)
+
+    row_first = (1 - (row + ROW_DEVICES - 1) // ROW_DEVICES) * (1 - z_hi)
+    col_first = 1 - (col + COL_DEVICES - 1) // COL_DEVICES
+    row_last, col_last = row == ROW_DEVICES - 1, col == COL_DEVICES - 1
+    row_by_post = jnp.logical_and(row_last, z_hi == 0)
+    half_way = ROW_DEVICES // 2
+    relay = (x_at, (row + half_way) % ROW_DEVICES, 0)
+    is_relay = col == 0
+    post = (x_at, half_way + col, 1)
+    post_col = row - half_way
+    is_post = jnp.logical_and(col == 1, jnp.logical_or(row == half_way, row == half_way + 1))
+    is_corner_post = jnp.logical_and(is_post, row % 2 == 1)
+    corner_by_post = jnp.logical_and(row_last, col == 0)
+    mail_corner = 1 - (1 - col_first) * (1 - row_first * core)
+    far_left = (x_at, relay[1], COL_DEVICES - 1)
+    far_corner = (x_at, (relay[1] + ROW_DEVICES - 1) % ROW_DEVICES, COL_DEVICES - 1)
+    far_above = (x_at, ROW_DEVICES - 1, post_col)
+    far_above_left = (x_at, ROW_DEVICES - 1, (post_col + COL_DEVICES - 1) % COL_DEVICES)
+
+    barrier = pltpu.get_barrier_semaphore()
+
+    def enter(*device):
+        pl.semaphore_signal(barrier, inc=1, device_id=device, device_id_type=MESH)
+
+    @pl.when(is_relay)
+    def _():
+        enter(*relay)
+        enter(*relay)
+        enter(*far_left)
+        enter(*far_corner)
+
+    @pl.when(is_post)
+    def _():
+        enter(x_at, 0, post_col)
+        enter(*far_above)
+
+    @pl.when(is_corner_post)
+    def _():
+        enter(x_at, 0, post_col)
+        enter(*far_above_left)
+
+    @pl.when(jnp.logical_not(row_by_post))
+    def _():
+        enter(x_at, below, col)
+
+    @pl.when(jnp.logical_not(col_last))
+    def _():
+        enter(x_at, row, right)
+
+    @pl.when(jnp.logical_not(jnp.logical_or(col_last, corner_by_post)))
+    def _():
+        enter(x_at, below, right)
+
+    near = [at_mate()]
+    near += [at_x((x_at + d) % NX) for d in range(1, NX)]
+    near += [at_y((y_at + d) % NY) for d in range(1, NY)]
+    near += [at_z((z_at + 1) % NZ), at_z((z_at + NZ - 1) % NZ)]
+    for partner in near:
+        enter(*partner)
+
     loads = [
         pltpu.make_async_copy(src, dst, in_sem.at[n])
         for n, (src, dst) in enumerate([
@@ -113,87 +195,6 @@
     for load in loads:
         load.start()
 
-    x_at, row, col = lax.axis_index("dp"), lax.axis_index("row"), lax.axis_index("col")
-    z_lo, y_at = row // NY, row % NY
-    z_hi, core = col // 2, col % 2
-    z_at = z_hi * NZ_LO + z_lo
-    mate = 1 - core
-
-    above = (row + ROW_DEVICES - 1) % ROW_DEVICES
-    below = (row + 1) % ROW_DEVICES
-    left = (col + COL_DEVICES - 1) % COL_DEVICES
-    right = (col + 1) % COL_DEVICES
-
-    def at_mate():
-        return (x_at, row, z_hi * 2 + mate)
-
-    def at_x(other):
-        return (other, row, col)
-
-    def at_y(other):
-        return (x_at, z_lo * NY + other, col)
-
-    def at_z(other):
-        return (x_at, (other % NZ_LO) * NY + y_at, (other // NZ_LO) * 2 + core)
-
-    row_first = 1 - (row + ROW_DEVICES - 1) // ROW_DEVICES
-    col_first = 1 - (col + COL_DEVICES - 1) // COL_DEVICES
-    row_last, col_last = row == ROW_DEVICES - 1, col == COL_DEVICES - 1
-    half_way = ROW_DEVICES // 2
-    relay = (x_at, (row + half_way) % ROW_DEVICES, 0)
-    is_relay = col == 0
-    post = (x_at, half_way + col, 1)
-    post_col = row - half_way
-    is_post = jnp.logical_and(col == 1, jnp.logical_and(row >= half_way, row < half_way + COL_DEVICES))
-    is_corner_post = jnp.logical_and(is_post, row % 2 == 1)
-    corner_by_post = jnp.logical_and(row_last, core == 0)
-    mail_corner = 1 - (1 - col_first) * (1 - row_first * core)
-    far_left = (x_at, relay[1], COL_DEVICES - 1)
-    far_corner = (x_at, (relay[1] + ROW_DEVICES - 1) % ROW_DEVICES, COL_DEVICES - 1)
-    far_above = (x_at, ROW_DEVICES - 1, post_col)
-    far_above_left = (x_at, ROW_DEVICES - 1, (post_col + COL_DEVICES - 1) % COL_DEVICES)
-
-    barrier = pltpu.get_barrier_semaphore()
-
-    def enter(*device):
-        pl.semaphore_signal(barrier, inc=1, device_id=device, device_id_type=MESH)
-
-    @pl.when(is_relay)
-    def _():
-        enter(*relay)
-        enter(*relay)
-        enter(*far_left)
-        enter(*far_corner)
-
-    @pl.when(is_post)
-    def _():
-        enter(x_at, 0, post_col)
-        enter(*far_above)
-
-    @pl.when(is_corner_post)
-    def _():
-        enter(x_at, 0, post_col)
-        enter(*far_above_left)
-
-    @pl.when(jnp.logical_not(row_last))
-    def _():
-        enter(x_at, below, col)
-
-    @pl.when(jnp.logical_not(col_last))
-    def _():
-        enter(x_at, row, right)
-
-    @pl.when(jnp.logical_not(jnp.logical_or(col_last, corner_by_post)))
-    def _():
-        enter(x_at, below, right)
-
-    near = [at_mate()]
-    near += [at_x((x_at + d) % NX) for d in range(1, NX)]
-    near += [at_y((y_at + d) % NY) for d in range(1, NY)]
-    near += [at_z((z_at + 1) % NZ), at_z((z_at + NZ - 1) % NZ)]
-    for partner in near:
-        enter(*partner)
-
     def spread_ring(n):
         for other in ((z_at + 2**n) % NZ, (z_at + NZ - 2**n) % NZ):
             pl.semaphore_signal(ring_sem.at[n], inc=1, device_id=at_z(other), device_id_type=MESH)
@@ -217,7 +218,7 @@
     stage_hid[...] = dot(pick, hid_ref[...]).astype(BF)
     stage_og[...] = dot(pick, og_ref[...]).astype(BF)
 
-    row_end, col_end = (row + 1) // ROW_DEVICES, (col + 1) // COL_DEVICES
+    row_end, col_end = (row + 1) // ROW_DEVICES * (1 - z_hi), (col + 1) // COL_DEVICES
     pl.semaphore_wait(barrier, 3 + len(near) + 2 * col_end + row_end + row_end * (1 - core))
 
     def go(*device):
@@ -228,7 +229,7 @@
         go(x_at, (row + half_way) % ROW_DEVICES, 0)
         go(x_at, (row + 1 + half_way) % ROW_DEVICES, 0)
 
-    @pl.when(row_last)
+    @pl.when(row_by_post)
     def _():
         go(*post)
 
@@ -495,13 +496,20 @@
     spread_ring(2)
 
     to_below, to_right, to_last = (x_at, below, col), (x_at, row, right), (x_at, below, right)
-    back = []
-    for n, (src, dst, device) in enumerate([
-        (back_rd.at[pl.ds(16, 16)], got_rd.at[pl.ds(16, 16)], to_last),
-        (back_rd.at[pl.ds(0, 16)], got_rd.at[pl.ds(0, 16)], to_right),
-        (back_main.at[pl.ds(128, 128)], got_up, to_below),
-    ]):
-        back.append(send(src, dst, back_ss.at[n], back_rs.at[n], device))
+    back = [
+        pltpu.make_async_remote_copy(
+            src_ref=src, dst_ref=dst, send_sem=back_ss.at[n], recv_sem=back_rs.at[n],
+            device_id=device, device_id_type=MESH,
+        )
+        for n, (src, dst, device) in enumerate([
+            (back_rd.at[pl.ds(16, 16)], got_rd.at[pl.ds(16, 16)], to_last),
+            (back_rd.at[pl.ds(0, 16)], got_rd.at[pl.ds(0, 16)], to_right),
+            (back_main.at[pl.ds(128, 128)], got_up, to_below),
+        ])
+    ]
+    back[0].start()
+    back[1].start()
+    pl.when(row_last)(back[2].start)
 
     first_parts, second_parts = [], []
     for b in (mlp, att):
@@ -528,6 +536,8 @@
         other = (x_at + d) % NX
         swaps.append(send(y3.at[other], ry3.at[d - 1], late_ss.at[2 + d], late_rs.at[2 + d], at_x(other)))
 
+    pl.when(jnp.logical_not(row_last))(back[2].start)
+
     for copy in swaps:
         copy.wait_recv()
     hear_ring(2)
@@ -598,6 +608,19 @@
         pltpu.VMEM((NX - 1, half, 128), BF),
         pltpu.VMEM((NY - 1, half, 128), BF),
     ]
+
+
+def finish_kernel(grad_in, att_in, mlp_in, grad_out, att_out, mlp_out, grad_s, att_s, mlp_s, in_sem, out_sem):
+    steps = ((grad_in, grad_s, grad_out), (att_in, att_s, att_out), (mlp_in, mlp_s, mlp_out))
+    loads = [pltpu.make_async_copy(src, held, in_sem.at[n]) for n, (src, held, _) in enumerate(steps)]
+    stores = [pltpu.make_async_copy(held, dst, out_sem.at[n]) for n, (_, held, dst) in enumerate(steps)]
+    for load in loads:
+        load.start()
+    for load, store in zip(loads, stores):
+        load.wait()
+        store.start()
+    for store in stores:
+        store.wait()
 
 
 def on_device(
@@ -669,6 +692,16 @@
         ),
         name="decoder_block_backward",
     )(*operands)
+    results = (grad_out, attention_grads, mlp_grads)
+    grad_out, attention_grads, mlp_grads = pl.pallas_call(
+        finish_kernel,
+        out_shape=tuple(jax.ShapeDtypeStruct(result.shape, result.dtype) for result in results),
+        in_specs=[pl.BlockSpec(memory_space=pltpu.HBM)] * 3,
+        out_specs=[pl.BlockSpec(memory_space=pltpu.HBM)] * 3,
+        scratch_shapes=[pltpu.VMEM(result.shape, result.dtype) for result in results] + [dma((3,)), dma((3,))],
+        compiler_params=pltpu.CompilerParams(vmem_limit_bytes=62 * 1024 * 1024),
+        name="hand_over_results",
+    )(*results)
     return grad_out.reshape(1, 8, 32, D), attention_grads, mlp_grads
 
 

time: 55.1 us -> 54.4 us (0.987)
  local copies, waits for them, and re-layouts: 2.84 us -> 0 us
  Pallas kernels: 51.5 us -> 53.6 us
    unnamed x7 -> x0, local copies, waits for them, and re-layouts: 2.84 us -> none
    pallas_call x0 -> x1, Pallas kernels: none -> 1.62 us  [on_device(): pl.pallas_call(finish_kernel, out_shape=tuple((jax.ShapeDtypeStruct(resul...]
    pallas_call x1, Pallas kernels: 51.5 us -> 52 us  [on_device(): pl.pallas_call(kernel, out_shape=(jax.ShapeDtypeStruct((CELLS, D), BF), j...]
where the time goes in v5:
time: 54.4 us; the launch traced here: 54.3 us
  Pallas kernels  53.6 us (99%)
  between operations  0.64 us (1%)
    pallas_call x1, Pallas kernels, on_device(): pl.pallas_call(kernel, out_shape=(jax.ShapeDtypeStruct((CELLS, D), BF), j...  52 us
    pallas_call x1, Pallas kernels, on_device(): pl.pallas_call(finish_kernel, out_shape=tuple((jax.ShapeDtypeStruct(resul...  1.62 us

profile of v5, /device:TPU:1, one launch (start us, length us, event | category | flops | bytes accessed | tf_op | source)
XLA Modules:
  0.0 54.3 jit_solution(4563397135469682592)
XLA Ops:
  0.6 52.0 %decoder_block_backward.1 = (bf16[256,256]{1,0:T(8,128)(2,1)}, f32[4,128]{1,0:T(4,128)}, f32[8,128]{1,0:T(8,128)}) custom-call(bf16[256,256]{1,0:T(8,128)(2,1)} %bitcast.6, s32[8,32]{1,0:T(8,128)} %bitcast.8, bf16[4,256]{1,0:T(4,128)(2,1)} %emb_in.1, f32[1,256]{1,0:T(1,128)} %bitcast.9, f32[1,256]{1,0:T(1,128)} %bitcast.10, bf16[256,768]{1,0:T(8,128)(2,1)} %wqkv_in.1, ...), custom_call_target="tpu_custom_call" | custom-call | tf_op jit(solution)/shard_map/decoder_block_backward/pallas_call | solution.py:644
  52.7 1.6 %hand_over_results.1 = (bf16[256,256]{1,0:T(8,128)(2,1)}, f32[4,128]{1,0:T(4,128)}, f32[8,128]{1,0:T(8,128)}) custom-call(bf16[256,256]{1,0:T(8,128)(2,1)} %get-tuple-element.9.grad_in, f32[4,128]{1,0:T(4,128)} %get-tuple-element.10.att_in, f32[8,128]{1,0:T(8,128)} %get-tuple-element.11.mlp_in), custom_call_target="tpu_custom_call" | custom-call | tf_op jit(solution)/shard_map/hand_over_results/pallas_call | solution.py:696

commit v6 on v5

--- a/solution.py
+++ b/solution.py
@@ -474,13 +474,13 @@
         dqkv_s[cells, D : 2 * D] = (own_heads(dot_tn(scores_low[cells], qkv_s[cells, :D])) * SCALE).astype(BF)
         dqkv_s[cells, 2 * D :] = own_heads(dot_tn(probs_low[cells], grad_context[cells])).astype(BF)
 
+    start_xy(mlp)
     for m in range(3):
         part_grad = dot_tn(normal_low, dqkv_s[:, D * m : D * (m + 1)])
         att_f32[0, pl.ds(m, 256, stride=3), :] = part_grad[:, :128]
         att_f32[1, pl.ds(m, 256, stride=3), :] = part_grad[:, 128:]
 
     start_mate(att)
-    start_xy(mlp)
 
     grad_norm_in = dot_nt(dqkv_s[...], wqkv_ref[...])
     grad_in = (grad_res + norm_back(grad_norm_in, normed_one, inv_one, gain_one)).astype(BF)
@@ -509,7 +509,7 @@
     ]
     back[0].start()
     back[1].start()
-    pl.when(row_last)(back[2].start)
+    back[2].start()
 
     first_parts, second_parts = [], []
     for b in (mlp, att):
@@ -536,7 +536,6 @@
         other = (x_at + d) % NX
         swaps.append(send(y3.at[other], ry3.at[d - 1], late_ss.at[2 + d], late_rs.at[2 + d], at_x(other)))
 
-    pl.when(jnp.logical_not(row_last))(back[2].start)
 
     for copy in swaps:
         copy.wait_recv()

time: 54.4 us -> 54.4 us (level)
  no operation moved by 1% of the time
where the time goes in v6:
time: 54.4 us; the launch traced here: 54.2 us
  Pallas kernels  53.6 us (99%)
  between operations  0.64 us (1%)
    pallas_call x1, Pallas kernels, on_device(): pl.pallas_call(kernel, out_shape=(jax.ShapeDtypeStruct((CELLS, D), BF), j...  52 us
    pallas_call x1, Pallas kernels, on_device(): pl.pallas_call(finish_kernel, out_shape=tuple((jax.ShapeDtypeStruct(resul...  1.62 us

profile of v6, /device:TPU:1, one launch (start us, length us, event | category | flops | bytes accessed | tf_op | source)
XLA Modules:
  0.0 54.2 jit_solution(4321965764631604746)
XLA Ops:
  0.6 52.0 %decoder_block_backward.1 = (bf16[256,256]{1,0:T(8,128)(2,1)}, f32[4,128]{1,0:T(4,128)}, f32[8,128]{1,0:T(8,128)}) custom-call(bf16[256,256]{1,0:T(8,128)(2,1)} %bitcast.6, s32[8,32]{1,0:T(8,128)} %bitcast.8, bf16[4,256]{1,0:T(4,128)(2,1)} %emb_in.1, f32[1,256]{1,0:T(1,128)} %bitcast.9, f32[1,256]{1,0:T(1,128)} %bitcast.10, bf16[256,768]{1,0:T(8,128)(2,1)} %wqkv_in.1, ...), custom_call_target="tpu_custom_call" | custom-call | tf_op jit(solution)/shard_map/decoder_block_backward/pallas_call | solution.py:643
  52.6 1.6 %hand_over_results.1 = (bf16[256,256]{1,0:T(8,128)(2,1)}, f32[4,128]{1,0:T(4,128)}, f32[8,128]{1,0:T(8,128)}) custom-call(bf16[256,256]{1,0:T(8,128)(2,1)} %get-tuple-element.9.grad_in, f32[4,128]{1,0:T(4,128)} %get-tuple-element.10.att_in, f32[8,128]{1,0:T(8,128)} %get-tuple-element.11.mlp_in), custom_call_target="tpu_custom_call" | custom-call | tf_op jit(solution)/shard_map/hand_over_results/pallas_call | solution.py:695

commit v7 on v6

--- a/solution.py
+++ b/solution.py
@@ -101,6 +101,7 @@
     att_f32, att_send, att_recv, att_x, att_y, att_rx, att_ry,
     x3, y3, rx3, ry3, z_send, z_recv, c_send, c_recv,
     in_sem, halo_ss, halo_rs, back_ss, back_rs, mlp_ss, mlp_rs, att_ss, att_rs, late_ss, late_rs, z_ss, z_rs, ring_sem, pass_ss, go_sem,
+    out_s, out_sem,
 ):
     x_at, row, col = lax.axis_index("dp"), lax.axis_index("row"), lax.axis_index("col")
     z_lo, y_at = row // NY, row % NY
@@ -178,8 +179,8 @@
         enter(x_at, below, right)
 
     near = [at_mate()]
-    near += [at_x((x_at + d) % NX) for d in range(1, NX)]
-    near += [at_y((y_at + d) % NY) for d in range(1, NY)]
+    near += [at_x((x_at + d) % NX) for d in (1, NX - 1)]
+    near += [at_y((y_at + d) % NY) for d in (1, NY - 1)]
     near += [at_z((z_at + 1) % NZ), at_z((z_at + NZ - 1) % NZ)]
     for partner in near:
         enter(*partner)
@@ -198,6 +199,13 @@
     def spread_ring(n):
         for other in ((z_at + 2**n) % NZ, (z_at + NZ - 2**n) % NZ):
             pl.semaphore_signal(ring_sem.at[n], inc=1, device_id=at_z(other), device_id_type=MESH)
+
+    def spread_plane():
+        for other in near[1:5]:
+            pl.semaphore_signal(ring_sem.at[3], inc=1, device_id=other, device_id_type=MESH)
+
+    def hear_plane():
+        pl.semaphore_wait(ring_sem.at[3], 4)
 
     def hear_ring(n):
         pl.semaphore_wait(ring_sem.at[n], 2)
@@ -283,6 +291,7 @@
     ]
 
     spread_ring(0)
+    spread_plane()
 
     loads[3].wait()
     rb = load_rel_bias(rb_ref[...])
@@ -474,6 +483,7 @@
         dqkv_s[cells, D : 2 * D] = (own_heads(dot_tn(scores_low[cells], qkv_s[cells, :D])) * SCALE).astype(BF)
         dqkv_s[cells, 2 * D :] = own_heads(dot_tn(probs_low[cells], grad_context[cells])).astype(BF)
 
+    hear_plane()
     start_xy(mlp)
     for m in range(3):
         part_grad = dot_tn(normal_low, dqkv_s[:, D * m : D * (m + 1)])
@@ -564,8 +574,10 @@
     for copy in back:
         copy.wait_recv()
     spread = one_hot(iota((128, 16), 0) == 32 * (iota((128, 16), 1) >> 2) + (iota((128, 16), 1) & 3))
-    out_ref[0:128, :] = (got_up[...].astype(F32) + dot(spread, got_rd[16:32, :])).astype(BF)
-    out_ref[128:256, :] = (back_main[0:128, :].astype(F32) + dot(spread, got_rd[0:16, :])).astype(BF)
+    out_s[0:128, :] = (got_up[...].astype(F32) + dot(spread, got_rd[16:32, :])).astype(BF)
+    out_s[128:256, :] = (back_main[0:128, :].astype(F32) + dot(spread, got_rd[0:16, :])).astype(BF)
+    out_copy = pltpu.make_async_copy(out_s, out_ref, out_sem)
+    out_copy.start()
 
     for copy in ring:
         copy.wait_recv()
@@ -585,6 +597,7 @@
     mlp_ref[...] = jnp.where(x_at < 2, apart, mixed)
     att_ref[...] = jnp.concatenate([first[4:5], second[4:5], first[5:6], second[5:6]], axis=0)
 
+    out_copy.wait()
     for copy in halo + back + sends + swaps + ring + [last]:
         copy.wait_send()
     for condition, _, steps in passes:
@@ -648,7 +661,7 @@
             jax.ShapeDtypeStruct((8, 128), F32),
         ),
         in_specs=[pl.BlockSpec(memory_space=pltpu.HBM)] * len(operands),
-        out_specs=[pl.BlockSpec(memory_space=pltpu.VMEM)] * 3,
+        out_specs=[pl.BlockSpec(memory_space=pltpu.HBM)] + [pl.BlockSpec(memory_space=pltpu.VMEM)] * 2,
         scratch_shapes=[pltpu.VMEM(operand.shape, operand.dtype) for operand in operands]
         + [
             pltpu.VMEM((32, D), BF),
@@ -685,7 +698,8 @@
         + [dma((len(operands),)), dma((9,)), dma((18,)), dma((3,)), dma((3,))]
         + [dma((7,))] * 6
         + [dma((NZ - 1,))] * 2
-        + [pltpu.SemaphoreType.REGULAR((3,)), dma((9,)), pltpu.SemaphoreType.REGULAR],
+        + [pltpu.SemaphoreType.REGULAR((4,)), dma((9,)), pltpu.SemaphoreType.REGULAR]
+        + [pltpu.VMEM((CELLS, D), BF), dma],
         compiler_params=pltpu.CompilerParams(
             collective_id=0, has_side_effects=True, vmem_limit_bytes=62 * 1024 * 1024
         ),

time: 54.4 us -> 54.2 us (level)
  no operation moved by 1% of the time
where the time goes in v7:
time: 54.2 us; the launch traced here: 54 us
  Pallas kernels  53.4 us (99%)
  between operations  0.64 us (1%)
    pallas_call x1, Pallas kernels, on_device(): pl.pallas_call(kernel, out_shape=(jax.ShapeDtypeStruct((CELLS, D), BF), j...  51.7 us
    pallas_call x1, Pallas kernels, on_device(): pl.pallas_call(finish_kernel, out_shape=tuple((jax.ShapeDtypeStruct(resul...  1.62 us

profile of v7, /device:TPU:1, one launch (start us, length us, event | category | flops | bytes accessed | tf_op | source)
XLA Modules:
  0.0 54.0 jit_solution(3705098594460183363)
XLA Ops:
  0.6 51.7 %decoder_block_backward.1 = (bf16[256,256]{1,0:T(8,128)(2,1)}, f32[4,128]{1,0:T(4,128)}, f32[8,128]{1,0:T(8,128)}) custom-call(bf16[256,256]{1,0:T(8,128)(2,1)} %bitcast.6, s32[8,32]{1,0:T(8,128)} %bitcast.8, bf16[4,256]{1,0:T(4,128)(2,1)} %emb_in.1, f32[1,256]{1,0:T(1,128)} %bitcast.9, f32[1,256]{1,0:T(1,128)} %bitcast.10, bf16[256,768]{1,0:T(8,128)(2,1)} %wqkv_in.1, ...), custom_call_target="tpu_custom_call" | custom-call | tf_op jit(solution)/shard_map/decoder_block_backward/pallas_call | solution.py:656
  52.4 1.6 %hand_over_results.1 = (bf16[256,256]{1,0:T(8,128)(2,1)}, f32[4,128]{1,0:T(4,128)}, f32[8,128]{1,0:T(8,128)}) custom-call(bf16[256,256]{1,0:T(8,128)(2,1)} %get-tuple-element.9.grad_in, f32[4,128]{1,0:T(4,128)} %get-tuple-element.10.att_in, f32[8,128]{1,0:T(8,128)} %get-tuple-element.11.mlp_in), custom_call_target="tpu_custom_call" | custom-call | tf_op jit(solution)/shard_map/hand_over_results/pallas_call | solution.py:709
